TPU v7x, 256 devices: a whole 4x4x8 slice. The times are simulated.
256 devices in a mesh: blk: 32 (over y_hi, z, core), uly: 8 (over x, y_lo).
Axes of the slice: x: 4, y: 4 (y_hi: 2, y_lo: 2; y = y_hi * 2 + y_lo), z: 8, core: 2. Of those that a mesh axis runs over, the one named last changes fastest.
Arguments:
- query_in: bfloat16 [32768, 2048], P(('blk', 'uly')), may hold values from -6 to 6
- key_in: bfloat16 [32768, 2048], P(('blk', 'uly')), may hold values from -6 to 6
- value_in: bfloat16 [32768, 2048], P(('blk', 'uly')), may hold values from -6 to 6
- out_grad: bfloat16 [32768, 2048], P(('blk', 'uly')), may hold values from -6 to 6
Outputs:
- attended: bfloat16 [32768, 2048], P(('blk', 'uly'))
- grad_query: bfloat16 [32768, 2048], P(('blk', 'uly'))
- grad_key: bfloat16 [32768, 2048], P(('blk', 'uly'))
- grad_value: bfloat16 [32768, 2048], P(('blk', 'uly'))
All inputs are finite; a program needn't handle non-finite values.
Results may differ from a plain program's by a relative error of at most 0.03.
Values may be sent and summed in bfloat16 or wider, within the bound.
A program may use at most 128 MiB of HBM per device.

v0:
```python
import jax
import jax.numpy as jnp
from jax import lax
from jax.sharding import PartitionSpec as P

HEADS = 16
HEAD_DIM = 128


def with_halo(block, sides, width):
    for axis, dim in sides:
        count = lax.axis_size(axis)
        forward = [(i, i + 1) for i in range(count - 1)]
        backward = [(target, source) for source, target in forward]
        low = lax.ppermute(
            lax.slice_in_dim(block, block.shape[dim] - width, None, axis=dim), axis, forward
        )
        high = lax.ppermute(lax.slice_in_dim(block, 0, width, axis=dim), axis, backward)
        block = jnp.concatenate([low, block, high], axis=dim)
    return block


def from_behind(array, axis, by):
    length = lax.axis_size(axis)
    pairs = [(i, i + by) for i in range(length) if 0 <= i + by < length]
    return lax.ppermute(array, axis, pairs)


def local(query_in, key_in, value_in, out_grad):
    ulysses = lax.axis_size("uly")
    cycle_size = lax.axis_size("blk")
    local_heads = HEADS // ulysses
    score_scale = HEAD_DIM ** (-0.5)
    query_flat, key_flat, value_flat, grad_flat = (
        lax.all_to_all(query_in, "uly", split_axis=1, concat_axis=0, tiled=True),
        lax.all_to_all(key_in, "uly", split_axis=1, concat_axis=0, tiled=True),
        lax.all_to_all(value_in, "uly", split_axis=1, concat_axis=0, tiled=True),
        lax.all_to_all(out_grad, "uly", split_axis=1, concat_axis=0, tiled=True),
    )
    row_count = query_flat.shape[0]
    place = lax.axis_index("blk")
    visible = [
        (place > 0).astype(jnp.float32),
        jnp.float32(1.0),
        (place < cycle_size - 1).astype(jnp.float32),
    ]

    def split_heads(matrix):
        return matrix.reshape(matrix.shape[0], local_heads, HEAD_DIM)

    def window_part(wide, index):
        return wide[:, index * row_count : (index + 1) * row_count]

    query_loc = split_heads(query_flat)
    grad_loc = split_heads(grad_flat)
    kv_wide = with_halo(jnp.stack([key_flat, value_flat]), (("blk", 1),), row_count)
    score_list = []
    row_max = jnp.full((row_count, local_heads), -jnp.inf, jnp.float32)
    for index in range(3):
        key_piece = split_heads(window_part(kv_wide, index)[0])
        scores = (
            jnp.einsum("qhd,khd->qhk", query_loc, key_piece, preferred_element_type=jnp.float32)
            * score_scale
        )
        score_list.append(scores)
        row_max = jnp.where(
            visible[index] > 0, jnp.maximum(row_max, jnp.max(scores, axis=2)), row_max
        )
    row_sum = jnp.zeros((row_count, local_heads), jnp.float32)
    for index in range(3):
        raised = jnp.where(
            visible[index] > 0, jnp.exp(score_list[index] - row_max[:, :, None]), 0.0
        )
        row_sum = row_sum + jnp.sum(raised, axis=2)
    log_norm = row_max + jnp.log(row_sum)
    weighted = jnp.zeros((row_count, local_heads, HEAD_DIM), jnp.float32)
    for index in range(3):
        value_piece = split_heads(window_part(kv_wide, index)[1])
        probas = jnp.where(
            visible[index] > 0, jnp.exp(score_list[index] - log_norm[:, :, None]), 0.0
        )
        weighted = weighted + jnp.einsum(
            "qhk,khd->qhd",
            probas.astype(jnp.bfloat16),
            value_piece,
            preferred_element_type=jnp.float32,
        )
    attended_loc = weighted.astype(jnp.bfloat16)
    row_dot = jnp.sum(grad_loc.astype(jnp.float32) * attended_loc.astype(jnp.float32), axis=2)
    parts = []
    for index in range(3):
        kv_piece = window_part(kv_wide, index)
        key_blk = split_heads(kv_piece[0])
        block_scores = (
            jnp.einsum("qhd,khd->qhk", query_loc, key_blk, preferred_element_type=jnp.float32)
            * score_scale
        )
        block_probas = jnp.where(
            visible[index] > 0, jnp.exp(block_scores - log_norm[:, :, None]), 0.0
        )
        weights = block_probas.astype(jnp.bfloat16)
        value_term = jnp.einsum(
            "qhk,qhd->khd", weights, grad_loc, preferred_element_type=jnp.float32
        )
        grad_probs = jnp.einsum(
            "qhd,khd->qhk", grad_loc, split_heads(kv_piece[1]), preferred_element_type=jnp.float32
        )
        grad_scores = (block_probas * (grad_probs - row_dot[:, :, None])).astype(jnp.bfloat16)
        query_term = jnp.einsum(
            "qhk,khd->qhd", grad_scores, key_blk, preferred_element_type=jnp.float32
        )
        key_term = jnp.einsum(
            "qhk,qhd->khd", grad_scores, query_loc, preferred_element_type=jnp.float32
        )
        parts.append(
            (
                query_term.reshape(row_count, -1),
                key_term.reshape(row_count, -1),
                value_term.reshape(row_count, -1),
            )
        )
    query_sum = parts[0][0] + parts[1][0] + parts[2][0]
    from_right = from_behind((parts[0][1], parts[0][2]), "blk", -1)
    from_left = (
        from_behind(parts[2][1].astype(jnp.bfloat16), "blk", 1).astype(jnp.float32),
        from_behind(parts[2][2].astype(jnp.bfloat16), "blk", 1).astype(jnp.float32),
    )
    key_sum = parts[1][1] + from_right[0] + from_left[0]
    value_sum = parts[1][2] + from_right[1] + from_left[1]
    query_grad = (query_sum * score_scale).astype(jnp.bfloat16)
    key_grad = (key_sum * score_scale).astype(jnp.bfloat16)
    value_grad = value_sum.astype(jnp.bfloat16)
    attended, grad_query, grad_key, grad_value = (
        lax.all_to_all(
            attended_loc.reshape(row_count, -1), "uly", split_axis=0, concat_axis=1, tiled=True
        ),
        lax.all_to_all(query_grad, "uly", split_axis=0, concat_axis=1, tiled=True),
        lax.all_to_all(key_grad, "uly", split_axis=0, concat_axis=1, tiled=True),
        lax.all_to_all(value_grad, "uly", split_axis=0, concat_axis=1, tiled=True),
    )
    return (attended, grad_query, grad_key, grad_value)


def solution(mesh):
    return jax.shard_map(
        local,
        mesh=mesh,
        in_specs=(
            P(("blk", "uly"), None),
            P(("blk", "uly"), None),
            P(("blk", "uly"), None),
            P(("blk", "uly"), None),
        ),
        out_specs=(
            P(("blk", "uly"), None),
            P(("blk", "uly"), None),
            P(("blk", "uly"), None),
            P(("blk", "uly"), None),
        ),
        check_vma=False,
    )
```

profile of v0, /device:TPU:16, one launch (start us, length us, event | category | flops | bytes accessed | tf_op | source)
XLA Modules:
  0.0 171.1 jit_solution(1978182236990745842)
XLA Ops:
  0.6 2.1 %copy.115 = bf16[128,2048]{0,1:T(8,128)(2,1)} copy(bf16[128,2048]{1,0:T(8,128)(2,1)} %param.5) | data formatting | bytes 1048576 | tf_op args[1]
  2.7 5.0 %all-to-all-start = ((bf16[128,8,256]{0,2,1:T(8,128)(2,1)}), bf16[128,8,256]{0,2,1:T(8,128)(2,1)S(1)}, u32[]{:S(2)}, u32[]{:S(2)}) async-start(bf16[128,8,256]{0,2,1:T(8,128)(2,1)} %bitcast), calls=%async_computation | async-start | bytes 1048576 | tf_op jit(solution)/shard_map/all_to_all | solution.py:36
  7.8 2.0 %copy.117 = bf16[128,2048]{0,1:T(8,128)(2,1)} copy(bf16[128,2048]{1,0:T(8,128)(2,1)} %param.6) | data formatting | bytes 1048576 | tf_op args[2]
  9.8 7.4 %all-to-all-done = bf16[128,8,256]{0,2,1:T(8,128)(2,1)S(1)} async-done(((bf16[128,8,256]{0,2,1:T(8,128)(2,1)}), bf16[128,8,256]{0,2,1:T(8,128)(2,1)S(1)}, u32[]{:S(2)}, u32[]{:S(2)}) %all-to-all-start) | async-done | bytes 524320 | tf_op jit(solution)/shard_map/all_to_all | solution.py:36
  17.2 3.5 %all-to-all-start.1 = ((bf16[128,8,256]{0,2,1:T(8,128)(2,1)}), bf16[128,8,256]{0,2,1:T(8,128)(2,1)S(1)}, u32[]{:S(2)}, u32[]{:S(2)}) async-start(bf16[128,8,256]{0,2,1:T(8,128)(2,1)} %bitcast.2), calls=%async_computation.1 | async-start | bytes 1048576 | tf_op jit(solution)/shard_map/all_to_all | solution.py:37
  20.7 2.0 %copy.119 = bf16[128,2048]{0,1:T(8,128)(2,1)} copy(bf16[128,2048]{1,0:T(8,128)(2,1)} %param.4) | data formatting | bytes 1048576 | tf_op args[0]
  22.8 6.8 %all-to-all-done.1 = bf16[128,8,256]{0,2,1:T(8,128)(2,1)S(1)} async-done(((bf16[128,8,256]{0,2,1:T(8,128)(2,1)}), bf16[128,8,256]{0,2,1:T(8,128)(2,1)S(1)}, u32[]{:S(2)}, u32[]{:S(2)}) %all-to-all-start.1) | async-done | bytes 524320 | tf_op jit(solution)/shard_map/all_to_all | solution.py:37
  29.6 3.5 %all-to-all-start.2 = ((bf16[128,8,256]{0,2,1:T(8,128)(2,1)}), bf16[128,8,256]{0,2,1:T(8,128)(2,1)S(1)}, u32[]{:S(2)}, u32[]{:S(2)}) async-start(bf16[128,8,256]{0,2,1:T(8,128)(2,1)} %bitcast.6), calls=%async_computation.2 | async-start | bytes 1048576 | tf_op jit(solution)/shard_map/all_to_all | solution.py:35
  35.9 6.4 %collective-permute-start.1 = (bf16[2,1024,256]{1,2,0:T(8,128)(2,1)}, bf16[2,1024,256]{1,2,0:T(8,128)(2,1)}, u32[]{:S(2)}, u32[]{:S(2)}) collective-permute-start(bf16[2,1024,256]{1,2,0:T(8,128)(2,1)} %constant_dynamic-update-slice_fusion), channel_id=1, source_target_pairs={{8,0},{16,8},{24,16},{32,24},{40,32},{48,40},{56,48},{64,56},{72,6... | collective-permute-start | bytes 3145736 | tf_op jit(solution)/shard_map/ppermute | solution.py:18
  43.4 6.0 %all-to-all-start.4 = ((bf16[128,8,256]{0,2,1:T(8,128)(2,1)}), bf16[128,8,256]{0,2,1:T(8,128)(2,1)S(1)}, u32[]{:S(2)}, u32[]{:S(2)}) async-start(bf16[128,8,256]{0,2,1:T(8,128)(2,1)} %bitcast.18), calls=%async_computation.4 | async-start | bytes 1048576 | tf_op jit(solution)/shard_map/all_to_all | solution.py:38
  49.4 1.9 %collective-permute-start = (bf16[2,1024,256]{1,2,0:T(8,128)(2,1)}, bf16[2,1024,256]{1,2,0:T(8,128)(2,1)}, u32[]{:S(2)}, u32[]{:S(2)}) collective-permute-start(bf16[2,1024,256]{1,2,0:T(8,128)(2,1)} %constant_dynamic-update-slice_fusion), channel_id=1, source_target_pairs={{0,8},{8,16},{16,24},{24,32},{32,40},{40,48},{48,56},{56,64},{64,7... | collective-permute-start | bytes 3145736 | tf_op jit(solution)/shard_map/ppermute | solution.py:15
  52.3 5.2 %all-to-all-done.4 = bf16[128,8,256]{0,2,1:T(8,128)(2,1)S(1)} async-done(((bf16[128,8,256]{0,2,1:T(8,128)(2,1)}), bf16[128,8,256]{0,2,1:T(8,128)(2,1)S(1)}, u32[]{:S(2)}, u32[]{:S(2)}) %all-to-all-start.4) | async-done | bytes 524320 | tf_op jit(solution)/shard_map/all_to_all | solution.py:38
  58.1 1.3 bitcast_reduce_fusion.1
  59.5 3.5 %fusion.52 = (bf16[1,1024,256]{1,2,0:T(8,128)(2,1)}, bf16[1,1024,256]{1,2,0:T(8,128)(2,1)S(1)}) fusion(bf16[2,1024,256]{1,2,0:T(8,128)(2,1)} %collective-permute-done.1), kind=kLoop, calls=%fused_computation.73 | loop fusion | bytes 2097152 | tf_op jit(solution)/shard_map/slice | solution.py:78
  63.0 1.3 bitcast_reduce_fusion
  64.3 5.1 %collective-permute-done = bf16[2,1024,256]{1,2,0:T(8,128)(2,1)} collective-permute-done((bf16[2,1024,256]{1,2,0:T(8,128)(2,1)}, bf16[2,1024,256]{1,2,0:T(8,128)(2,1)}, u32[]{:S(2)}, u32[]{:S(2)}) %collective-permute-start) | collective-permute-done | bytes 1048608 | tf_op jit(solution)/shard_map/ppermute | solution.py:15
  69.4 2.1 %fusion.53 = (bf16[1,1024,256]{1,2,0:T(8,128)(2,1)}, bf16[1,1024,256]{1,2,0:T(8,128)(2,1)S(1)}) fusion(bf16[2,1024,256]{1,2,0:T(8,128)(2,1)} %collective-permute-done), kind=kLoop, calls=%fused_computation.74 | loop fusion | bytes 2097152 | tf_op jit(solution)/shard_map/slice | solution.py:78
  72.3 1.3 bitcast_reduce_fusion.2
  73.6 4.9 %fusion.12 = (f32[1024,2]{0,1:T(2,128)S(1)}, f32[1024,2]{0,1:T(2,128)S(1)}, f32[1024,2]{0,1:T(2,128)S(1)}) fusion(f32[2,1024,1024]{2,1,0:T(8,128)S(1)} %get-tuple-element.22, f32[1024,2]{0,1:T(2,128)S(1)} %maximum_select_fusion, f32[2,1024,1024]{2,1,0:T(8,128)S(1)} %get-tuple-element.20, pred[]{:T(512)S(6)} %gt.8, ...), kind=kLoop, calls=%fused_computation.21 | loop fusion | flops 23062528 | bytes 25198594 | tf_op jit(solution)/shard_map/reduce_sum | solution.py:74
  78.5 2.7 %fusion.39 = f32[2,1024,128]{1,2,0:T(8,128)} fusion(bf16[1024,2,128]{0,2,1:T(8,128)(2,1)S(1)} %reshape.101, f32[2,1024,1024]{2,1,0:T(8,128)S(1)} %get-tuple-element.24, f32[1024,2]{0,1:T(2,128)S(1)} %log_add_fusion, pred[]{:T(512)S(6)} %gt.7), kind=kOutput, calls=%fused_computation.58 | convolution fusion | flops 545259520 | bytes 9969665 | tf_op jit(solution)/shard_map/qhk,qhd->khd/dot_general | solution.py:102
  81.2 2.5 %convolution_convert_fusion = bf16[2,1024,128]{1,2,0:T(8,128)(2,1)} fusion(bf16[1024,2,128]{0,2,1:T(8,128)(2,1)S(1)} %reshape.101, f32[2,1024,1024]{2,1,0:T(8,128)S(1)} %get-tuple-element.20, f32[1024,2]{0,1:T(2,128)S(1)} %log_add_fusion, pred[]{:T(512)S(6)} %gt.8), kind=kOutput, calls=%fused_computation.46 | convolution fusion | flops 545521664 | bytes 9445377 | tf_op jit(solution)/shard_map/qhk,qhd->khd/dot_general | solution.py:102
  83.7 1.6 convolution_bitcast_fusion.1
  85.3 1.8 %fusion.26 = f32[1024,2,128]{0,2,1:T(8,128)S(1)} fusion(f32[1024,2,128]{0,2,1:T(8,128)S(1)} %convolution_bitcast_fusion.1, bf16[1024,2,128]{0,2,1:T(8,128)(2,1)S(1)} %bitcast.228, f32[2,1024,1024]{2,1,0:T(8,128)S(1)} %get-tuple-element.24, f32[1024,2]{0,1:T(2,128)S(1)} %log_add_fusion, pred[]{:T(512)S(6)} %gt.7), kind=kOutput, calls=%fused_computation.44 | convolution fusion | flops 545521664 | bytes 11018241 | tf_op jit(solution)/shard_map/qhk,khd->qhd/dot_general | solution.py:82
  87.2 2.6 %multiply_reduce_fusion = (f32[1024,2]{0,1:T(2,128)S(1)}, bf16[1024,2,128]{0,2,1:T(8,128)(2,1)}) fusion(bf16[1024,2,128]{0,2,1:T(8,128)(2,1)S(1)} %reshape.101, f32[1024,2,128]{0,2,1:T(8,128)S(1)} %fusion.26, bf16[1024,2,128]{0,2,1:T(8,128)(2,1)S(1)} %bitcast.226, f32[2,1024,1024]{2,1,0:T(8,128)S(1)} %get-tuple-element.20, f32[1024,2]{0,1:T(2,128)S(1)} %log_add_fusion, ...), kind=kOutput, calls=%fused_computation.56 | convolution fusion | flops 546830336 | bytes 11026433 | tf_op jit(solution)/shard_map/qhk,khd->qhd/dot_general | solution.py:82
  89.7 3.7 %fusion.1 = bf16[1024,2,1024]{0,2,1:T(8,128)(2,1)} fusion(f32[2,1024,1024]{2,1,0:T(8,128)S(1)} %get-tuple-element.20, f32[1024,2]{0,1:T(2,128)S(1)} %get-tuple-element.25, f32[1024,2]{0,1:T(2,128)S(1)} %log_add_fusion, pred[]{:T(512)S(6)} %gt.8, bf16[1024,2,128]{0,2,1:T(8,128)(2,1)S(1)} %bitcast.227, bf16[1024,2,128]{0,2,1:T(8,128)(2,1)S(1)} %reshape.101), kind=kOutput, calls=%fused_computation.2 | convolution fusion | flops 549453824 | bytes 13647873 | tf_op jit(solution)/shard_map/qhd,khd->qhk/dot_general | solution.py:105
  93.4 2.5 %fusion.5 = bf16[1024,2,1024]{0,2,1:T(8,128)(2,1)S(1)} fusion(f32[2,1024,1024]{2,1,0:T(8,128)S(1)} %get-tuple-element.24, f32[1024,2]{0,1:T(2,128)S(1)} %get-tuple-element.25, f32[1024,2]{0,1:T(2,128)S(1)} %log_add_fusion, pred[]{:T(512)S(6)} %gt.7, bf16[1024,2,128]{0,2,1:T(8,128)(2,1)S(1)} %bitcast.229, bf16[1024,2,128]{0,2,1:T(8,128)(2,1)S(1)} %reshape.101), kind=kOutput, calls=%fused_computation.8 | convolution fusion | flops 549453824 | bytes 13647873 | tf_op jit(solution)/shard_map/qhd,khd->qhk/dot_general | solution.py:105
  95.9 2.4 %fusion.3 = bf16[1024,2,1024]{0,2,1:T(8,128)(2,1)S(1)} fusion(f32[2,1024,1024]{2,1,0:T(8,128)S(1)} %get-tuple-element.22, f32[1024,2]{0,1:T(2,128)S(1)} %get-tuple-element.25, f32[1024,2]{0,1:T(2,128)S(1)} %log_add_fusion, bf16[1024,2,128]{0,2,1:T(8,128)(2,1)S(1)} %reshape_squeeze_stack.9, bf16[1024,2,128]{0,2,1:T(8,128)(2,1)S(1)} %reshape.101), kind=kOutput, calls=%fused_computation.5 | convolution fusion | flops 547356672 | bytes 13647872 | tf_op jit(solution)/shard_map/qhd,khd->qhk/dot_general | solution.py:105
  98.3 2.1 %collective-permute-start.4 = (f32[1024,256]{0,1:T(8,128)}, f32[1024,256]{0,1:T(8,128)}, u32[]{:S(2)}, u32[]{:S(2)}) collective-permute-start(f32[1024,256]{0,1:T(8,128)} %bitcast.40), channel_id=1, source_target_pairs={{8,0},{16,8},{24,16},{32,24},{40,32},{48,40},{56,48},{64,56},{72,6... | collective-permute-start | bytes 3145736 | tf_op jit(solution)/shard_map/ppermute | solution.py:26
  100.4 2.4 %collective-permute-start.5 = (bf16[1024,256]{0,1:T(8,128)(2,1)}, bf16[1024,256]{0,1:T(8,128)(2,1)}, u32[]{:S(2)}, u32[]{:S(2)}) collective-permute-start(bf16[1024,256]{0,1:T(8,128)(2,1)} %bitcast.42), channel_id=1, source_target_pairs={{0,8},{8,16},{16,24},{24,32},{32,40},{40,48},{48,56},{56,64},{64,7... | collective-permute-start | bytes 1572872 | tf_op jit(solution)/shard_map/ppermute | solution.py:26
  102.8 2.5 %fusion.55 = f32[2,1024,128]{1,2,0:T(8,128)} fusion(bf16[1024,2,1024]{0,2,1:T(8,128)(2,1)S(1)} %fusion.5, bf16[1024,2,128]{0,2,1:T(8,128)(2,1)S(1)} %reshape.100), kind=kOutput, calls=%fused_computation.76 | convolution fusion | flops 536870912 | bytes 5767168 | tf_op jit(solution)/shard_map/qhk,qhd->khd/dot_general | solution.py:112
  105.3 7.0 %collective-permute-start.2 = (f32[1024,256]{0,1:T(8,128)}, f32[1024,256]{0,1:T(8,128)}, u32[]{:S(2)}, u32[]{:S(2)}) collective-permute-start(f32[1024,256]{0,1:T(8,128)} %bitcast.31), channel_id=1, source_target_pairs={{8,0},{16,8},{24,16},{32,24},{40,32},{48,40},{56,48},{64,56},{72,6... | collective-permute-start | bytes 3145736 | tf_op jit(solution)/shard_map/ppermute | solution.py:26
  115.7 5.7 %all-to-all-start.5 = ((bf16[8,128,256]{1,2,0:T(8,128)(2,1)}), bf16[8,128,256]{1,2,0:T(8,128)(2,1)S(1)}, u32[]{:S(2)}, u32[]{:S(2)}) async-start(bf16[8,128,256]{1,2,0:T(8,128)(2,1)} %copy.146), calls=%async_computation.5 | async-start | bytes 1048576 | tf_op jit(solution)/shard_map/all_to_all | solution.py:137
  121.4 5.1 %fusion.34 = f32[2,1024,128]{1,2,0:T(8,128)S(1)} fusion(bf16[1024,2,128]{0,2,1:T(8,128)(2,1)S(1)} %reshape.101, f32[2,1024,1024]{2,1,0:T(8,128)} %copy-done, f32[1024,2]{0,1:T(2,128)S(1)} %log_add_fusion), kind=kOutput, calls=%fused_computation.57 | convolution fusion | flops 543162368 | bytes 9969664 | tf_op jit(solution)/shard_map/qhk,qhd->khd/dot_general | solution.py:102
  127.4 2.1 %all-to-all-done.5 = bf16[8,128,256]{1,2,0:T(8,128)(2,1)S(1)} async-done(((bf16[8,128,256]{1,2,0:T(8,128)(2,1)}), bf16[8,128,256]{1,2,0:T(8,128)(2,1)S(1)}, u32[]{:S(2)}, u32[]{:S(2)}) %all-to-all-start.5) | async-done | bytes 524320 | tf_op jit(solution)/shard_map/all_to_all | solution.py:137
  129.5 3.6 %all-to-all-start.3 = ((bf16[8,128,256]{1,2,0:T(8,128)(2,1)}), bf16[8,128,256]{1,2,0:T(8,128)(2,1)S(1)}, u32[]{:S(2)}, u32[]{:S(2)}) async-start(bf16[8,128,256]{1,2,0:T(8,128)(2,1)} %copy.132), calls=%async_computation.3 | async-start | bytes 1048576 | tf_op jit(solution)/shard_map/all_to_all | solution.py:134
  133.1 4.5 %convolution_convert_fusion.1 = bf16[2,1024,128]{1,2,0:T(8,128)(2,1)} fusion(bf16[1024,2,1024]{0,2,1:T(8,128)(2,1)} %fusion.1, bf16[1024,2,128]{0,2,1:T(8,128)(2,1)S(1)} %reshape.100), kind=kOutput, calls=%fused_computation.47 | convolution fusion | flops 537133056 | bytes 5242880 | tf_op jit(solution)/shard_map/qhk,qhd->khd/dot_general | solution.py:112
  137.7 1.9 %collective-permute-start.3 = (bf16[1024,256]{0,1:T(8,128)(2,1)}, bf16[1024,256]{0,1:T(8,128)(2,1)}, u32[]{:S(2)}, u32[]{:S(2)}) collective-permute-start(bf16[1024,256]{0,1:T(8,128)(2,1)} %bitcast.33), channel_id=1, source_target_pairs={{0,8},{8,16},{16,24},{24,32},{32,40},{40,48},{48,56},{56,64},{64,7... | collective-permute-start | bytes 1572872 | tf_op jit(solution)/shard_map/ppermute | solution.py:26
  139.6 1.5 fusion.30
  142.2 5.7 %all-to-all-start.7 = ((bf16[8,128,256]{2,1,0:T(8,128)(2,1)}), bf16[8,128,256]{2,1,0:T(8,128)(2,1)S(1)}, u32[]{:S(2)}, u32[]{:S(2)}) async-start(bf16[8,128,256]{2,1,0:T(8,128)(2,1)} %bitcast.43), calls=%async_computation.7 | async-start | bytes 1048576 | tf_op jit(solution)/shard_map/all_to_all | solution.py:139
  147.9 3.7 %fusion.54 = f32[2,1024,128]{1,2,0:T(8,128)S(1)} fusion(bf16[1024,2,1024]{0,2,1:T(8,128)(2,1)} %copy-done.1, bf16[1024,2,128]{0,2,1:T(8,128)(2,1)S(1)} %reshape.100), kind=kOutput, calls=%fused_computation.75 | convolution fusion | flops 536870912 | bytes 5767168 | tf_op jit(solution)/shard_map/qhk,qhd->khd/dot_general | solution.py:112
  151.6 2.3 %collective-permute-done.3 = bf16[1024,256]{0,1:T(8,128)(2,1)} collective-permute-done((bf16[1024,256]{0,1:T(8,128)(2,1)}, bf16[1024,256]{0,1:T(8,128)(2,1)}, u32[]{:S(2)}, u32[]{:S(2)}) %collective-permute-start.3) | collective-permute-done | bytes 524320 | tf_op jit(solution)/shard_map/ppermute | solution.py:26
  153.8 1.6 fusion.33
  156.4 5.2 %all-to-all-start.6 = ((bf16[8,128,256]{2,1,0:T(8,128)(2,1)}), bf16[8,128,256]{2,1,0:T(8,128)(2,1)S(1)}, u32[]{:S(2)}, u32[]{:S(2)}) async-start(bf16[8,128,256]{2,1,0:T(8,128)(2,1)} %bitcast.34), calls=%async_computation.6 | async-start | bytes 1048576 | tf_op jit(solution)/shard_map/all_to_all | solution.py:138
  161.7 1.0 copy.158
  162.7 1.0 copy.157
  163.9 1.0 copy.160
  165.0 4.9 %all-to-all-done.6 = bf16[8,128,256]{2,1,0:T(8,128)(2,1)S(1)} async-done(((bf16[8,128,256]{2,1,0:T(8,128)(2,1)}), bf16[8,128,256]{2,1,0:T(8,128)(2,1)S(1)}, u32[]{:S(2)}, u32[]{:S(2)}) %all-to-all-start.6) | async-done | bytes 524320 | tf_op jit(solution)/shard_map/all_to_all | solution.py:138
  170.1 1.0 copy.159
  (55 shorter events, 13.0 us)
Async XLA Ops:
  0.6 41.7 %copy-start.7 = (bf16[128,2048]{1,0:T(8,128)(2,1)S(1)}, bf16[128,2048]{1,0:T(8,128)(2,1)}, u32[]{:S(2)}) copy-start(bf16[128,2048]{1,0:T(8,128)(2,1)} %param.7) | copy-start | bytes 1572868
  2.7 14.5 %all-to-all-start = ((bf16[128,8,256]{0,2,1:T(8,128)(2,1)}), bf16[128,8,256]{0,2,1:T(8,128)(2,1)S(1)}, u32[]{:S(2)}, u32[]{:S(2)}) async-start(bf16[128,8,256]{0,2,1:T(8,128)(2,1)} %bitcast), calls=%async_computation | async-start | bytes 1048576 | tf_op jit(solution)/shard_map/all_to_all | solution.py:36
  17.2 12.4 %all-to-all-start.1 = ((bf16[128,8,256]{0,2,1:T(8,128)(2,1)}), bf16[128,8,256]{0,2,1:T(8,128)(2,1)S(1)}, u32[]{:S(2)}, u32[]{:S(2)}) async-start(bf16[128,8,256]{0,2,1:T(8,128)(2,1)} %bitcast.2), calls=%async_computation.1 | async-start | bytes 1048576 | tf_op jit(solution)/shard_map/all_to_all | solution.py:37
  29.6 13.7 %all-to-all-start.2 = ((bf16[128,8,256]{0,2,1:T(8,128)(2,1)}), bf16[128,8,256]{0,2,1:T(8,128)(2,1)S(1)}, u32[]{:S(2)}, u32[]{:S(2)}) async-start(bf16[128,8,256]{0,2,1:T(8,128)(2,1)} %bitcast.6), calls=%async_computation.2 | async-start | bytes 1048576 | tf_op jit(solution)/shard_map/all_to_all | solution.py:35
  35.9 23.5 %collective-permute-start.1 = (bf16[2,1024,256]{1,2,0:T(8,128)(2,1)}, bf16[2,1024,256]{1,2,0:T(8,128)(2,1)}, u32[]{:S(2)}, u32[]{:S(2)}) collective-permute-start(bf16[2,1024,256]{1,2,0:T(8,128)(2,1)} %constant_dynamic-update-slice_fusion), channel_id=1, source_target_pairs={{8,0},{16,8},{24,16},{32,24},{40,32},{48,40},{56,48},{64,56},{72,6... | collective-permute-start | bytes 3145736 | tf_op jit(solution)/shard_map/ppermute | solution.py:18
  43.4 14.2 %all-to-all-start.4 = ((bf16[128,8,256]{0,2,1:T(8,128)(2,1)}), bf16[128,8,256]{0,2,1:T(8,128)(2,1)S(1)}, u32[]{:S(2)}, u32[]{:S(2)}) async-start(bf16[128,8,256]{0,2,1:T(8,128)(2,1)} %bitcast.18), calls=%async_computation.4 | async-start | bytes 1048576 | tf_op jit(solution)/shard_map/all_to_all | solution.py:38
  49.4 20.0 %collective-permute-start = (bf16[2,1024,256]{1,2,0:T(8,128)(2,1)}, bf16[2,1024,256]{1,2,0:T(8,128)(2,1)}, u32[]{:S(2)}, u32[]{:S(2)}) collective-permute-start(bf16[2,1024,256]{1,2,0:T(8,128)(2,1)} %constant_dynamic-update-slice_fusion), channel_id=1, source_target_pairs={{0,8},{8,16},{16,24},{24,32},{32,40},{40,48},{48,56},{56,64},{64,7... | collective-permute-start | bytes 3145736 | tf_op jit(solution)/shard_map/ppermute | solution.py:15
  59.4 36.4 %copy-start = (f32[2,1024,1024]{2,1,0:T(8,128)}, f32[2,1024,1024]{2,1,0:T(8,128)S(1)}, u32[]{:S(2)}) copy-start(f32[2,1024,1024]{2,1,0:T(8,128)S(1)} %get-tuple-element.22) | copy-start | bytes 25165828
  63.0 8.5 %copy-start.3 = (bf16[1,1024,256]{1,2,0:T(8,128)(2,1)}, bf16[1,1024,256]{1,2,0:T(8,128)(2,1)S(1)}, u32[]{:S(2)}) copy-start(bf16[1,1024,256]{1,2,0:T(8,128)(2,1)S(1)} %get-tuple-element.16) | copy-start | bytes 1572868
  71.5 0.8 copy-start.5
  81.2 4.1 %copy-start.10 = (bf16[1,1024,256]{1,2,0:T(8,128)(2,1)S(1)}, bf16[1,1024,256]{1,2,0:T(8,128)(2,1)}, u32[]{:S(2)}) copy-start(bf16[1,1024,256]{1,2,0:T(8,128)(2,1)} %get-tuple-element.17) | copy-start | bytes 1572868
  85.3 1.9 %copy-start.9 = (bf16[1,1024,256]{1,2,0:T(8,128)(2,1)S(1)}, bf16[1,1024,256]{1,2,0:T(8,128)(2,1)}, u32[]{:S(2)}) copy-start(bf16[1,1024,256]{1,2,0:T(8,128)(2,1)} %get-tuple-element.15) | copy-start | bytes 1572868
  98.3 15.6 %copy-start.1 = (bf16[1024,2,1024]{0,2,1:T(8,128)(2,1)}, bf16[1024,2,1024]{0,2,1:T(8,128)(2,1)S(1)}, u32[]{:S(2)}) copy-start(bf16[1024,2,1024]{0,2,1:T(8,128)(2,1)S(1)} %fusion.3) | copy-start | bytes 12582916
  98.3 14.8 %copy-start.6 = (bf16[1,1024,256]{1,2,0:T(8,128)(2,1)S(1)}, bf16[1,1024,256]{1,2,0:T(8,128)(2,1)}, u32[]{:S(2)}) copy-start(bf16[1,1024,256]{1,2,0:T(8,128)(2,1)} %copy-done.5) | copy-start | bytes 1572868
  98.3 41.3 %collective-permute-start.4 = (f32[1024,256]{0,1:T(8,128)}, f32[1024,256]{0,1:T(8,128)}, u32[]{:S(2)}, u32[]{:S(2)}) collective-permute-start(f32[1024,256]{0,1:T(8,128)} %bitcast.40), channel_id=1, source_target_pairs={{8,0},{16,8},{24,16},{32,24},{40,32},{48,40},{56,48},{64,56},{72,6... | collective-permute-start | bytes 3145736 | tf_op jit(solution)/shard_map/ppermute | solution.py:26
  100.4 39.2 %collective-permute-start.5 = (bf16[1024,256]{0,1:T(8,128)(2,1)}, bf16[1024,256]{0,1:T(8,128)(2,1)}, u32[]{:S(2)}, u32[]{:S(2)}) collective-permute-start(bf16[1024,256]{0,1:T(8,128)(2,1)} %bitcast.42), channel_id=1, source_target_pairs={{0,8},{8,16},{16,24},{24,32},{32,40},{40,48},{48,56},{56,64},{64,7... | collective-permute-start | bytes 1572872 | tf_op jit(solution)/shard_map/ppermute | solution.py:26
  105.3 8.6 %copy-start.2 = (bf16[1024,2,1024]{0,2,1:T(8,128)(2,1)S(1)}, bf16[1024,2,1024]{0,2,1:T(8,128)(2,1)}, u32[]{:S(2)}) copy-start(bf16[1024,2,1024]{0,2,1:T(8,128)(2,1)} %fusion.1) | copy-start | bytes 12582916
  105.3 8.6 %copy-start.4 = (bf16[1,1024,256]{1,2,0:T(8,128)(2,1)S(1)}, bf16[1,1024,256]{1,2,0:T(8,128)(2,1)}, u32[]{:S(2)}) copy-start(bf16[1,1024,256]{1,2,0:T(8,128)(2,1)} %copy-done.3) | copy-start | bytes 1572868
  105.3 48.6 %collective-permute-start.2 = (f32[1024,256]{0,1:T(8,128)}, f32[1024,256]{0,1:T(8,128)}, u32[]{:S(2)}, u32[]{:S(2)}) collective-permute-start(f32[1024,256]{0,1:T(8,128)} %bitcast.31), channel_id=1, source_target_pairs={{8,0},{16,8},{24,16},{32,24},{40,32},{48,40},{56,48},{64,56},{72,6... | collective-permute-start | bytes 3145736 | tf_op jit(solution)/shard_map/ppermute | solution.py:26
  113.9 12.6 %copy-start.8 = (bf16[1024,2,128]{0,2,1:T(8,128)(2,1)S(1)}, bf16[1024,2,128]{0,2,1:T(8,128)(2,1)}, u32[]{:S(2)}) copy-start(bf16[1024,2,128]{0,2,1:T(8,128)(2,1)} %get-tuple-element.26) | copy-start | bytes 1572868
  115.7 13.9 %all-to-all-start.5 = ((bf16[8,128,256]{1,2,0:T(8,128)(2,1)}), bf16[8,128,256]{1,2,0:T(8,128)(2,1)S(1)}, u32[]{:S(2)}, u32[]{:S(2)}) async-start(bf16[8,128,256]{1,2,0:T(8,128)(2,1)} %copy.146), calls=%async_computation.5 | async-start | bytes 1048576 | tf_op jit(solution)/shard_map/all_to_all | solution.py:137
  129.5 12.6 %all-to-all-start.3 = ((bf16[8,128,256]{1,2,0:T(8,128)(2,1)}), bf16[8,128,256]{1,2,0:T(8,128)(2,1)S(1)}, u32[]{:S(2)}, u32[]{:S(2)}) async-start(bf16[8,128,256]{1,2,0:T(8,128)(2,1)} %copy.132), calls=%async_computation.3 | async-start | bytes 1048576 | tf_op jit(solution)/shard_map/all_to_all | solution.py:134
  137.7 16.2 %collective-permute-start.3 = (bf16[1024,256]{0,1:T(8,128)(2,1)}, bf16[1024,256]{0,1:T(8,128)(2,1)}, u32[]{:S(2)}, u32[]{:S(2)}) collective-permute-start(bf16[1024,256]{0,1:T(8,128)(2,1)} %bitcast.33), channel_id=1, source_target_pairs={{0,8},{8,16},{16,24},{24,32},{32,40},{40,48},{48,56},{56,64},{64,7... | collective-permute-start | bytes 1572872 | tf_op jit(solution)/shard_map/ppermute | solution.py:26
  142.2 14.3 %all-to-all-start.7 = ((bf16[8,128,256]{2,1,0:T(8,128)(2,1)}), bf16[8,128,256]{2,1,0:T(8,128)(2,1)S(1)}, u32[]{:S(2)}, u32[]{:S(2)}) async-start(bf16[8,128,256]{2,1,0:T(8,128)(2,1)} %bitcast.43), calls=%async_computation.7 | async-start | bytes 1048576 | tf_op jit(solution)/shard_map/all_to_all | solution.py:139
  156.4 13.4 %all-to-all-start.6 = ((bf16[8,128,256]{2,1,0:T(8,128)(2,1)}), bf16[8,128,256]{2,1,0:T(8,128)(2,1)S(1)}, u32[]{:S(2)}, u32[]{:S(2)}) async-start(bf16[8,128,256]{2,1,0:T(8,128)(2,1)} %bitcast.34), calls=%async_computation.6 | async-start | bytes 1048576 | tf_op jit(solution)/shard_map/all_to_all | solution.py:138
where the time goes:
time: 172 us; the launch traced here: 171 us
  starting transfers between devices  60 us (35%)
  matrix products  41.7 us (24%)
  waiting for transfers between devices  33.8 us (20%)
  local copies, waits for them, and re-layouts  26.5 us (15%)
  other arithmetic  8.02 us (5%)
    ppermute x4, starting transfers between devices, from_behind(): return lax.ppermute(array, axis, pairs)  13.4 us
    unnamed x33, local copies, waits for them, and re-layouts  13.1 us
    dot_general x3, matrix products, local(): jnp.einsum('qhk,qhd->khd', grad_scores, query_loc, preferred_element_type...  10.7 us
    dot_general x3, matrix products, local(): jnp.einsum('qhk,qhd->khd', weights, grad_loc, preferred_element_type=jnp....  10.3 us
    dot_general x3, matrix products, local(): jnp.einsum('qhd,khd->qhk', grad_loc, split_heads(kv_piece[1]), preferred_...  8.52 us
    all_to_all x1, waiting for transfers between devices, local(): lax.all_to_all(key_in, 'uly', split_axis=1, concat_axis=0, tiled=True)  7.43 us
    all_to_all x1, waiting for transfers between devices, local(): lax.all_to_all(value_in, 'uly', split_axis=1, concat_axis=0, tiled=True)  6.85 us
    ppermute x1, starting transfers between devices, with_halo(): lax.ppermute(lax.slice_in_dim(block, 0, width, axis=dim), axis, backward)  6.39 us
  transfers between devices with their start and end apart: 14, of which 7 were waited for; matrix products, arithmetic and copies ran while one was open for 26% of the time, Pallas kernels for 0%

commit v1 on v0

v1 whole, which is shorter than its diff:
```python
import jax
import jax.numpy as jnp
from jax import lax
from jax.experimental import pallas as pl
from jax.experimental.pallas import tpu as pltpu
from jax.sharding import PartitionSpec as P

HEADS = 16
HEAD_DIM = 128
SCALE = HEAD_DIM ** (-0.5)
LOG2_SCALE = SCALE * 1.4426950408889634
MESH = pl.DeviceIdType.MESH
CHUNK = 512
Q, K, V, G = range(4)
O, DQ, DK, DV = range(4)


def dot(a, b):
    return jnp.dot(a, b, preferred_element_type=jnp.float32)


def kernel(
    q_in, k_in, v_in, g_in, o_out, dq_out, dk_out, dv_out,
    q_buf, g_buf, k_buf, v_buf, scores, weights, o_buf, dq_buf, dk_buf, dv_buf,
    own_dk, own_dv, edge_out, edge_in,
    in_send, in_recv, halo_send, halo_recv, edge_send, edge_recv, out_send, out_recv,
):
    rows = q_in.shape[0]
    block = q_buf.shape[1]
    blocks = lax.axis_size("blk")
    width = lax.axis_size("uly")
    place = lax.axis_index("blk")
    member = lax.axis_index("uly")
    has_left = place > 0
    has_right = place < blocks - 1
    column_x, column_y = lax.div(member, 2), lax.rem(member, 2)
    inputs, outputs = (q_in, k_in, v_in, g_in), (o_out, dq_out, dk_out, dv_out)

    def peer(r):
        x = lax.rem(column_x + lax.div(r, 2), width // 2)
        y = lax.rem(column_y + lax.rem(r, 2), 2)
        return x * 2 + y

    def each_peer(body):
        lax.fori_loop(1, width, lambda r, _: (body(jnp.int32(r)), 0)[1], 0)

    barrier = pltpu.get_barrier_semaphore()
    each_peer(
        lambda r: pl.semaphore_signal(
            barrier, inc=1, device_id=(place, peer(r)), device_id_type=MESH
        )
    )

    @pl.when(has_left)
    def _():
        pl.semaphore_signal(barrier, inc=1, device_id=(place - 1, member), device_id_type=MESH)

    @pl.when(has_right)
    def _():
        pl.semaphore_signal(barrier, inc=1, device_id=(place + 1, member), device_id_type=MESH)

    pl.semaphore_wait(
        barrier, width - 1 + has_left.astype(jnp.int32) + has_right.astype(jnp.int32)
    )

    def columns(owner, h):
        return pl.ds(pl.multiple_of((owner * 2 + h) * HEAD_DIM, HEAD_DIM), HEAD_DIM)

    def token_rows(owner):
        return pl.ds(pl.multiple_of(owner * rows, rows), rows)

    def in_place(a, h):
        if a == Q:
            return q_buf.at[h, token_rows(member)]
        if a == G:
            return g_buf.at[h, token_rows(member)]
        buf = k_buf if a == K else v_buf
        return buf.at[h, 1, token_rows(member)]

    def in_copy(a, h, r):
        return pltpu.make_async_remote_copy(
            src_ref=inputs[a].at[:, columns(peer(r), h)],
            dst_ref=in_place(a, h),
            send_sem=in_send.at[a, h, r],
            recv_sem=in_recv.at[a, h, r],
            device_id=(place, peer(r)),
            device_id_type=MESH,
        )

    def in_own(a, h):
        return pltpu.make_async_copy(
            inputs[a].at[:, columns(member, h)], in_place(a, h), in_recv.at[a, h, 0]
        )

    def send_in(a, h):
        each_peer(lambda r: in_copy(a, h, r).start())
        in_own(a, h).start()

    def wait_in(a, h):
        each_peer(lambda r: in_copy(a, h, r).wait_recv())
        in_own(a, h).wait()

    def pair_copies(src, dst, send, recv):
        right = pltpu.make_async_remote_copy(
            src_ref=src[0], dst_ref=dst[0], send_sem=send[0], recv_sem=recv[0],
            device_id=(place + 1, member), device_id_type=MESH,
        )
        left = pltpu.make_async_remote_copy(
            src_ref=src[1], dst_ref=dst[1], send_sem=send[1], recv_sem=recv[1],
            device_id=(place - 1, member), device_id_type=MESH,
        )
        return right, left

    def halo(a, h):
        buf, i = (k_buf, 0) if a == K else (v_buf, 1)
        own = buf.at[h, 1]
        return pair_copies(
            (own, own), (buf.at[h, 0], buf.at[h, 2]),
            (halo_send.at[i, h, 0], halo_send.at[i, h, 1]),
            (halo_recv.at[i, h, 0], halo_recv.at[i, h, 1]),
        )

    def edge(i, h):
        return pair_copies(
            (edge_out.at[i, h, 0], edge_out.at[i, h, 1]),
            (edge_in.at[i, h, 0], edge_in.at[i, h, 1]),
            (edge_send.at[i, h, 0], edge_send.at[i, h, 1]),
            (edge_recv.at[i, h, 0], edge_recv.at[i, h, 1]),
        )

    def start_pair(pair):
        right, left = pair
        pl.when(has_right)(right.start)
        pl.when(has_left)(left.start)

    def wait_recv_pair(pair):
        right, left = pair
        pl.when(has_left)(right.wait_recv)
        pl.when(has_right)(left.wait_recv)

    def wait_send_pair(pair):
        right, left = pair
        pl.when(has_right)(right.wait_send)
        pl.when(has_left)(left.wait_send)

    results = (o_buf, dq_buf, dk_buf, dv_buf)

    def out_copy(i, h, r):
        return pltpu.make_async_remote_copy(
            src_ref=results[i].at[h, token_rows(peer(r))],
            dst_ref=outputs[i].at[:, columns(member, h)],
            send_sem=out_send.at[i, h, r],
            recv_sem=out_recv.at[i, h, r],
            device_id=(place, peer(r)),
            device_id_type=MESH,
        )

    def out_own(i, h):
        return pltpu.make_async_copy(
            results[i].at[h, token_rows(member)],
            outputs[i].at[:, columns(member, h)],
            out_recv.at[i, h, 0],
        )

    def send_out(i, h):
        each_peer(lambda r: out_copy(i, h, r).start())
        out_own(i, h).start()

    for a in (K, Q, V, G):
        send_in(a, 0)

    @pl.when(jnp.logical_not(has_left))
    def _():
        k_buf[:, 0] = jnp.zeros_like(k_buf[:, 0])
        v_buf[:, 0] = jnp.zeros_like(v_buf[:, 0])
        edge_in[:, :, 0] = jnp.zeros_like(edge_in[:, :, 0])

    @pl.when(jnp.logical_not(has_right))
    def _():
        k_buf[:, 2] = jnp.zeros_like(k_buf[:, 2])
        v_buf[:, 2] = jnp.zeros_like(v_buf[:, 2])
        edge_in[:, :, 1] = jnp.zeros_like(edge_in[:, :, 1])

    seen = (has_left, None, has_right)
    per_slot = block // CHUNK

    def piece(c):
        return slice(c * CHUNK, (c + 1) * CHUNK)

    def slot_scores(h, slot, query_t):
        best = jnp.full((8, block), -jnp.inf, jnp.float32)
        for c in range(per_slot):
            part = dot(k_buf[h, slot, piece(c)], query_t)
            scores[slot, piece(c)] = part
            best = jnp.maximum(best, jnp.max(part.reshape(CHUNK // 8, 8, block), axis=0))
        if seen[slot] is not None:
            best = jnp.where(seen[slot], best, -jnp.inf)
        return best

    def slot_weights(h, slot, top):
        if seen[slot] is not None:
            top = jnp.where(seen[slot], top, jnp.float32(1e30))
        total = jnp.zeros((8, block), jnp.float32)
        acc = jnp.zeros((HEAD_DIM, block), jnp.float32)
        for c in range(per_slot):
            raised = jnp.exp2(scores[slot, piece(c)] * LOG2_SCALE - top)
            total = total + jnp.sum(raised.reshape(CHUNK // 8, 8, block), axis=0)
            low = raised.astype(jnp.bfloat16)
            weights[slot, piece(c)] = low
            acc = acc + dot(v_buf[h, slot, piece(c)].T, low)
        return total, acc

    def slot_grads(h, slot, query, grad, grad_t, row_dot, dk_ref, dv_ref):
        acc = jnp.zeros((HEAD_DIM, block), jnp.float32)
        for c in range(per_slot):
            low = weights[slot, piece(c)]
            grad_probs = dot(v_buf[h, slot, piece(c)], grad_t)
            grad_scores = (low.astype(jnp.float32) * (grad_probs - row_dot)).astype(jnp.bfloat16)
            dv_ref[piece(c)] = dot(low, grad).astype(dv_ref.dtype)
            dk_ref[piece(c)] = dot(grad_scores, query).astype(dk_ref.dtype)
            acc = acc + dot(k_buf[h, slot, piece(c)].T, grad_scores)
        return acc

    def finish_keys(h):
        for i, (own, buf, scale) in enumerate(((own_dk, dk_buf, SCALE), (own_dv, dv_buf, 1.0))):
            wait_recv_pair(edge(i, h))
            total = (
                own[h]
                + edge_in[i, h, 0].astype(jnp.float32)
                + edge_in[i, h, 1].astype(jnp.float32)
            )
            buf[h] = (total * scale).astype(jnp.bfloat16)
            send_out(DK + i, h)

    for h in range(2):
        if h == 0:
            wait_in(K, 0)
            start_pair(halo(K, 0))
            send_in(K, 1)
        wait_in(Q, h)
        query = q_buf[h]
        query_t = query.T
        best = slot_scores(h, 1, query_t)
        if h == 0:
            wait_in(V, 0)
            start_pair(halo(V, 0))
            send_in(Q, 1)
            send_in(V, 1)
            send_in(G, 1)
        wait_recv_pair(halo(K, h))
        for slot in (0, 2):
            best = jnp.maximum(best, slot_scores(h, slot, query_t))
        if h == 1:
            finish_keys(0)
        wait_recv_pair(halo(V, h))
        top = jnp.max(best, axis=0, keepdims=True) * LOG2_SCALE
        total, acc = slot_weights(h, 1, top)
        for slot in (0, 2):
            more, term = slot_weights(h, slot, top)
            total, acc = total + more, acc + term
        inverse = 1.0 / jnp.sum(total, axis=0, keepdims=True)
        attended_t = (acc * inverse).astype(jnp.bfloat16)
        o_buf[h] = attended_t.T
        send_out(O, h)
        if h == 0:
            wait_in(K, 1)
            start_pair(halo(K, 1))
        wait_in(G, h)
        grad_t = (g_buf[h].T.astype(jnp.float32) * inverse).astype(jnp.bfloat16)
        row_dot = jnp.sum(
            grad_t.astype(jnp.float32) * attended_t.astype(jnp.float32), axis=0, keepdims=True
        )
        grad = grad_t.T
        acc = slot_grads(
            h, 2, query, grad, grad_t, row_dot, edge_out.at[0, h, 0], edge_out.at[1, h, 0]
        )
        acc = acc + slot_grads(
            h, 0, query, grad, grad_t, row_dot, edge_out.at[0, h, 1], edge_out.at[1, h, 1]
        )
        start_pair(edge(0, h))
        start_pair(edge(1, h))
        if h == 0:
            wait_in(V, 1)
            start_pair(halo(V, 1))
        acc = acc + slot_grads(h, 1, query, grad, grad_t, row_dot, own_dk.at[h], own_dv.at[h])
        dq_buf[h] = (acc * SCALE).astype(jnp.bfloat16).T
        send_out(DQ, h)
    finish_keys(1)

    for h in range(2):
        for a in range(4):
            each_peer(lambda r: in_copy(a, h, r).wait_send())
        for i in range(2):
            wait_send_pair(halo((K, V)[i], h))
            wait_send_pair(edge(i, h))
        for i in range(4):
            each_peer(lambda r: out_copy(i, h, r).wait())
            out_own(i, h).wait()


def local(query_in, key_in, value_in, out_grad):
    width = lax.axis_size("uly")
    rows, _ = query_in.shape
    block = rows * width
    heads = HEADS // width
    low, full = jnp.bfloat16, jnp.float32
    dma = pltpu.SemaphoreType.DMA
    whole = pl.BlockSpec(memory_space=pl.ANY)
    return pl.pallas_call(
        kernel,
        in_specs=[whole] * 4,
        out_specs=[whole] * 4,
        out_shape=[jax.ShapeDtypeStruct(query_in.shape, low)] * 4,
        scratch_shapes=[
            pltpu.VMEM((heads, block, HEAD_DIM), low),
            pltpu.VMEM((heads, block, HEAD_DIM), low),
            pltpu.VMEM((heads, 3, block, HEAD_DIM), low),
            pltpu.VMEM((heads, 3, block, HEAD_DIM), low),
            pltpu.VMEM((3, block, block), full),
            pltpu.VMEM((3, block, block), low),
            pltpu.VMEM((heads, block, HEAD_DIM), low),
            pltpu.VMEM((heads, block, HEAD_DIM), low),
            pltpu.VMEM((heads, block, HEAD_DIM), low),
            pltpu.VMEM((heads, block, HEAD_DIM), low),
            pltpu.VMEM((heads, block, HEAD_DIM), full),
            pltpu.VMEM((heads, block, HEAD_DIM), full),
            pltpu.VMEM((2, heads, 2, block, HEAD_DIM), low),
            pltpu.VMEM((2, heads, 2, block, HEAD_DIM), low),
            dma((4, heads, width)),
            dma((4, heads, width)),
            dma((2, heads, 2)),
            dma((2, heads, 2)),
            dma((2, heads, 2)),
            dma((2, heads, 2)),
            dma((4, heads, width)),
            dma((4, heads, width)),
        ],
        compiler_params=pltpu.CompilerParams(
            collective_id=0, has_side_effects=True, vmem_limit_bytes=60 * 2**20
        ),
        cost_estimate=pl.CostEstimate(
            flops=12 * heads * 3 * block * block * HEAD_DIM,
            bytes_accessed=16 * rows * HEADS * HEAD_DIM,
            transcendentals=heads * 3 * block * block,
        ),
    )(query_in, key_in, value_in, out_grad)


def solution(mesh):
    spec = P(("blk", "uly"), None)
    return jax.shard_map(
        local,
        mesh=mesh,
        in_specs=(spec,) * 4,
        out_specs=(spec,) * 4,
        check_vma=False,
    )
```

time: 172 us -> 95.7 us (0.56)
  the two profiles are of different devices: /device:TPU:16 before, /device:TPU:217 now
where the time goes in v1:
time: 95.7 us; the launch traced here: 95.5 us
  Pallas kernels  89.6 us (94%)
  local copies, waits for them, and re-layouts  5.19 us (5%)
    pallas_call x1, Pallas kernels, local(): pl.pallas_call(kernel, in_specs=[whole] * 4, out_specs=[whole] * 4, out_s...  89.6 us
    unnamed x10, local copies, waits for them, and re-layouts  5.19 us

profile of v1, /device:TPU:217, one launch (start us, length us, event | category | flops | bytes accessed | tf_op | source)
XLA Modules:
  0.0 95.5 jit_solution(12356052591461245002)
XLA Ops:
  0.6 89.6 %shard_map.75 = (bf16[128,2048]{1,0:T(8,128)(2,1)}, bf16[128,2048]{1,0:T(8,128)(2,1)}, bf16[128,2048]{1,0:T(8,128)(2,1)}, bf16[128,2048]{1,0:T(8,128)(2,1)}) custom-call(bf16[128,2048]{1,0:T(8,128)(2,1)} %q_in.1, bf16[128,2048]{1,0:T(8,128)(2,1)} %k_in.1, bf16[128,2048]{1,0:T(8,128)(2,1)} %v_in.1, bf16[128,2048]{1,0:T(8,128)(2,1)} %g_in.1), custom_call_target="tpu_custom_call" | custom-call | flops 9663676416 | bytes 4194304 | tf_op jit(solution)/shard_map/pallas_call | solution.py:309
  90.3 0.0 copy-start.2
  90.3 1.9 %copy.12 = bf16[128,2048]{1,0:T(8,128)(2,1)} copy(bf16[128,2048]{1,0:T(8,128)(2,1)} %get-tuple-element.8) | data formatting | bytes 1048576
  92.2 0.0 copy-done.2
  92.2 0.0 copy-start.1
  92.2 0.8 copy.13
  93.0 0.4 copy-done.1
  93.4 0.0 copy-start
  93.4 0.8 copy.14
  94.2 0.4 copy-done
  94.7 0.8 copy.15
Async XLA Ops:
  90.3 2.0 %copy-start.2 = (bf16[128,2048]{1,0:T(8,128)(2,1)S(1)}, bf16[128,2048]{1,0:T(8,128)(2,1)}, u32[]{:S(2)}) copy-start(bf16[128,2048]{1,0:T(8,128)(2,1)} %get-tuple-element.9) | copy-start | bytes 1572868
  92.2 1.2 %copy-start.1 = (bf16[128,2048]{1,0:T(8,128)(2,1)S(1)}, bf16[128,2048]{1,0:T(8,128)(2,1)}, u32[]{:S(2)}) copy-start(bf16[128,2048]{1,0:T(8,128)(2,1)} %get-tuple-element.10) | copy-start | bytes 1572868
  93.4 1.2 %copy-start = (bf16[128,2048]{1,0:T(8,128)(2,1)S(1)}, bf16[128,2048]{1,0:T(8,128)(2,1)}, u32[]{:S(2)}) copy-start(bf16[128,2048]{1,0:T(8,128)(2,1)} %get-tuple-element.11) | copy-start | bytes 1572868

commit v2 on v1

--- a/solution.py
+++ b/solution.py
@@ -41,6 +41,17 @@
         y = lax.rem(column_y + lax.rem(r, 2), 2)
         return x * 2 + y
 
+    def flipped(owner):
+        return owner + 1 - 2 * lax.rem(owner, 2)
+
+    upper = place >= blocks // 2
+
+    def heads_of(owner):
+        return jnp.where(upper, flipped(owner), owner)
+
+    right = (place + 1, jnp.where(place == blocks // 2 - 1, flipped(member), member))
+    left = (place - 1, jnp.where(place == blocks // 2, flipped(member), member))
+
     def each_peer(body):
         lax.fori_loop(1, width, lambda r, _: (body(jnp.int32(r)), 0)[1], 0)
 
@@ -53,18 +64,18 @@
 
     @pl.when(has_left)
     def _():
-        pl.semaphore_signal(barrier, inc=1, device_id=(place - 1, member), device_id_type=MESH)
+        pl.semaphore_signal(barrier, inc=1, device_id=left, device_id_type=MESH)
 
     @pl.when(has_right)
     def _():
-        pl.semaphore_signal(barrier, inc=1, device_id=(place + 1, member), device_id_type=MESH)
+        pl.semaphore_signal(barrier, inc=1, device_id=right, device_id_type=MESH)
 
     pl.semaphore_wait(
         barrier, width - 1 + has_left.astype(jnp.int32) + has_right.astype(jnp.int32)
     )
 
     def columns(owner, h):
-        return pl.ds(pl.multiple_of((owner * 2 + h) * HEAD_DIM, HEAD_DIM), HEAD_DIM)
+        return pl.ds(pl.multiple_of((heads_of(owner) * 2 + h) * HEAD_DIM, HEAD_DIM), HEAD_DIM)
 
     def token_rows(owner):
         return pl.ds(pl.multiple_of(owner * rows, rows), rows)
@@ -101,15 +112,15 @@
         in_own(a, h).wait()
 
     def pair_copies(src, dst, send, recv):
-        right = pltpu.make_async_remote_copy(
+        to_right = pltpu.make_async_remote_copy(
             src_ref=src[0], dst_ref=dst[0], send_sem=send[0], recv_sem=recv[0],
-            device_id=(place + 1, member), device_id_type=MESH,
-        )
-        left = pltpu.make_async_remote_copy(
+            device_id=right, device_id_type=MESH,
+        )
+        to_left = pltpu.make_async_remote_copy(
             src_ref=src[1], dst_ref=dst[1], send_sem=send[1], recv_sem=recv[1],
-            device_id=(place - 1, member), device_id_type=MESH,
-        )
-        return right, left
+            device_id=left, device_id_type=MESH,
+        )
+        return to_right, to_left
 
     def halo(a, h):
         buf, i = (k_buf, 0) if a == K else (v_buf, 1)
@@ -129,19 +140,19 @@
         )
 
     def start_pair(pair):
-        right, left = pair
-        pl.when(has_right)(right.start)
-        pl.when(has_left)(left.start)
+        to_right, to_left = pair
+        pl.when(has_right)(to_right.start)
+        pl.when(has_left)(to_left.start)
 
     def wait_recv_pair(pair):
-        right, left = pair
-        pl.when(has_left)(right.wait_recv)
-        pl.when(has_right)(left.wait_recv)
+        to_right, to_left = pair
+        pl.when(has_left)(to_right.wait_recv)
+        pl.when(has_right)(to_left.wait_recv)
 
     def wait_send_pair(pair):
-        right, left = pair
-        pl.when(has_right)(right.wait_send)
-        pl.when(has_left)(left.wait_send)
+        to_right, to_left = pair
+        pl.when(has_right)(to_right.wait_send)
+        pl.when(has_left)(to_left.wait_send)
 
     results = (o_buf, dq_buf, dk_buf, dv_buf)
 
@@ -298,6 +309,19 @@
             out_own(i, h).wait()
 
 
+def hand_over(*refs):
+    sources, targets, (held, fetched, stored) = refs[:4], refs[4:8], refs[8:]
+    fetch = [pltpu.make_async_copy(sources[i], held.at[i], fetched.at[i]) for i in range(4)]
+    store = [pltpu.make_async_copy(held.at[i], targets[i], stored.at[i]) for i in range(4)]
+    for copy in fetch:
+        copy.start()
+    for i in range(4):
+        fetch[i].wait()
+        store[i].start()
+    for copy in store:
+        copy.wait()
+
+
 def local(query_in, key_in, value_in, out_grad):
     width = lax.axis_size("uly")
     rows, _ = query_in.shape
@@ -306,7 +330,7 @@
     low, full = jnp.bfloat16, jnp.float32
     dma = pltpu.SemaphoreType.DMA
     whole = pl.BlockSpec(memory_space=pl.ANY)
-    return pl.pallas_call(
+    results = pl.pallas_call(
         kernel,
         in_specs=[whole] * 4,
         out_specs=[whole] * 4,
@@ -344,6 +368,13 @@
             transcendentals=heads * 3 * block * block,
         ),
     )(query_in, key_in, value_in, out_grad)
+    return pl.pallas_call(
+        hand_over,
+        in_specs=[whole] * 4,
+        out_specs=[whole] * 4,
+        out_shape=[jax.ShapeDtypeStruct(query_in.shape, low)] * 4,
+        scratch_shapes=[pltpu.VMEM((4, *query_in.shape), low), dma((4,)), dma((4,))],
+    )(*results)
 
 
 def solution(mesh):

time: 95.7 us -> 70.5 us (0.74)
  the two profiles are of different devices: /device:TPU:217 before, /device:TPU:16 now
where the time goes in v2:
time: 70.5 us; the launch traced here: 70.4 us
  Pallas kernels  69.6 us (99%)
  between operations  0.8 us (1%)
    pallas_call x1, Pallas kernels, local(): pl.pallas_call(kernel, in_specs=[whole] * 4, out_specs=[whole] * 4, out_s...  67.2 us
    pallas_call x1, Pallas kernels, local(): pl.pallas_call(hand_over, in_specs=[whole] * 4, out_specs=[whole] * 4, ou...  2.42 us

profile of v2, /device:TPU:16, one launch (start us, length us, event | category | flops | bytes accessed | tf_op | source)
XLA Modules:
  0.0 70.4 jit_solution(9761854958518346720)
XLA Ops:
  0.6 67.2 %shard_map.75 = (bf16[128,2048]{1,0:T(8,128)(2,1)}, bf16[128,2048]{1,0:T(8,128)(2,1)}, bf16[128,2048]{1,0:T(8,128)(2,1)}, bf16[128,2048]{1,0:T(8,128)(2,1)}) custom-call(bf16[128,2048]{1,0:T(8,128)(2,1)} %q_in.1, bf16[128,2048]{1,0:T(8,128)(2,1)} %k_in.1, bf16[128,2048]{1,0:T(8,128)(2,1)} %v_in.1, bf16[128,2048]{1,0:T(8,128)(2,1)} %g_in.1), custom_call_target="tpu_custom_call" | custom-call | flops 9663676416 | bytes 4194304 | tf_op jit(solution)/shard_map/pallas_call | solution.py:333
  67.8 2.4 %shard_map.76 = (bf16[128,2048]{1,0:T(8,128)(2,1)}, bf16[128,2048]{1,0:T(8,128)(2,1)}, bf16[128,2048]{1,0:T(8,128)(2,1)}, bf16[128,2048]{1,0:T(8,128)(2,1)}) custom-call(bf16[128,2048]{1,0:T(8,128)(2,1)} %get-tuple-element.8.refs_0_, bf16[128,2048]{1,0:T(8,128)(2,1)} %get-tuple-element.9.refs_1_, bf16[128,2048]{1,0:T(8,128)(2,1)} %get-tuple-element.10.refs_2_, ...), custom_call_target="tpu_custom_call" | custom-call | tf_op jit(solution)/shard_map/pallas_call | solution.py:371

commit v3 on v2

--- a/solution.py
+++ b/solution.py
@@ -13,6 +13,7 @@
 CHUNK = 512
 Q, K, V, G = range(4)
 O, DQ, DK, DV = range(4)
+FAR, CORE, OWN = range(3)
 
 
 def dot(a, b):
@@ -31,8 +32,7 @@
     width = lax.axis_size("uly")
     place = lax.axis_index("blk")
     member = lax.axis_index("uly")
-    has_left = place > 0
-    has_right = place < blocks - 1
+    core = lax.rem(place, 2)
     column_x, column_y = lax.div(member, 2), lax.rem(member, 2)
     inputs, outputs = (q_in, k_in, v_in, g_in), (o_out, dq_out, dk_out, dv_out)
 
@@ -49,8 +49,16 @@
     def heads_of(owner):
         return jnp.where(upper, flipped(owner), owner)
 
-    right = (place + 1, jnp.where(place == blocks // 2 - 1, flipped(member), member))
-    left = (place - 1, jnp.where(place == blocks // 2, flipped(member), member))
+    far = place + 2 * core - 1
+    has_far = jnp.logical_and(far >= 0, far < blocks)
+    crosses = jnp.logical_or(
+        jnp.logical_and(place == blocks // 2 - 1, core == 1),
+        jnp.logical_and(place == blocks // 2, core == 0),
+    )
+    sides = (
+        (far, jnp.where(crosses, flipped(member), member)),
+        (place + 1 - 2 * core, member),
+    )
 
     def each_peer(body):
         lax.fori_loop(1, width, lambda r, _: (body(jnp.int32(r)), 0)[1], 0)
@@ -61,18 +69,13 @@
             barrier, inc=1, device_id=(place, peer(r)), device_id_type=MESH
         )
     )
-
-    @pl.when(has_left)
+    pl.semaphore_signal(barrier, inc=1, device_id=sides[CORE], device_id_type=MESH)
+
+    @pl.when(has_far)
     def _():
-        pl.semaphore_signal(barrier, inc=1, device_id=left, device_id_type=MESH)
-
-    @pl.when(has_right)
-    def _():
-        pl.semaphore_signal(barrier, inc=1, device_id=right, device_id_type=MESH)
-
-    pl.semaphore_wait(
-        barrier, width - 1 + has_left.astype(jnp.int32) + has_right.astype(jnp.int32)
-    )
+        pl.semaphore_signal(barrier, inc=1, device_id=sides[FAR], device_id_type=MESH)
+
+    pl.semaphore_wait(barrier, width + has_far.astype(jnp.int32))
 
     def columns(owner, h):
         return pl.ds(pl.multiple_of((heads_of(owner) * 2 + h) * HEAD_DIM, HEAD_DIM), HEAD_DIM)
@@ -86,7 +89,7 @@
         if a == G:
             return g_buf.at[h, token_rows(member)]
         buf = k_buf if a == K else v_buf
-        return buf.at[h, 1, token_rows(member)]
+        return buf.at[h, OWN, token_rows(member)]
 
     def in_copy(a, h, r):
         return pltpu.make_async_remote_copy(
@@ -111,48 +114,40 @@
         each_peer(lambda r: in_copy(a, h, r).wait_recv())
         in_own(a, h).wait()
 
-    def pair_copies(src, dst, send, recv):
-        to_right = pltpu.make_async_remote_copy(
-            src_ref=src[0], dst_ref=dst[0], send_sem=send[0], recv_sem=recv[0],
-            device_id=right, device_id_type=MESH,
-        )
-        to_left = pltpu.make_async_remote_copy(
-            src_ref=src[1], dst_ref=dst[1], send_sem=send[1], recv_sem=recv[1],
-            device_id=left, device_id_type=MESH,
-        )
-        return to_right, to_left
-
-    def halo(a, h):
+    def halo(a, h, side):
         buf, i = (k_buf, 0) if a == K else (v_buf, 1)
-        own = buf.at[h, 1]
-        return pair_copies(
-            (own, own), (buf.at[h, 0], buf.at[h, 2]),
-            (halo_send.at[i, h, 0], halo_send.at[i, h, 1]),
-            (halo_recv.at[i, h, 0], halo_recv.at[i, h, 1]),
-        )
-
-    def edge(i, h):
-        return pair_copies(
-            (edge_out.at[i, h, 0], edge_out.at[i, h, 1]),
-            (edge_in.at[i, h, 0], edge_in.at[i, h, 1]),
-            (edge_send.at[i, h, 0], edge_send.at[i, h, 1]),
-            (edge_recv.at[i, h, 0], edge_recv.at[i, h, 1]),
-        )
-
-    def start_pair(pair):
-        to_right, to_left = pair
-        pl.when(has_right)(to_right.start)
-        pl.when(has_left)(to_left.start)
-
-    def wait_recv_pair(pair):
-        to_right, to_left = pair
-        pl.when(has_left)(to_right.wait_recv)
-        pl.when(has_right)(to_left.wait_recv)
-
-    def wait_send_pair(pair):
-        to_right, to_left = pair
-        pl.when(has_right)(to_right.wait_send)
-        pl.when(has_left)(to_left.wait_send)
+        return pltpu.make_async_remote_copy(
+            src_ref=buf.at[h, OWN],
+            dst_ref=buf.at[h, side],
+            send_sem=halo_send.at[i, h, side],
+            recv_sem=halo_recv.at[i, h, side],
+            device_id=sides[side],
+            device_id_type=MESH,
+        )
+
+    def edge(i, h, side):
+        return pltpu.make_async_remote_copy(
+            src_ref=edge_out.at[i, h, side],
+            dst_ref=edge_in.at[i, h, side],
+            send_sem=edge_send.at[i, h, side],
+            recv_sem=edge_recv.at[i, h, side],
+            device_id=sides[side],
+            device_id_type=MESH,
+        )
+
+    def if_there(side, action):
+        if side == FAR:
+            pl.when(has_far)(action)
+        else:
+            action()
+
+    def start_halo(a, h):
+        for side in (FAR, CORE):
+            if_there(side, halo(a, h, side).start)
+
+    def start_edges(h, side):
+        for i in range(2):
+            if_there(side, edge(i, h, side).start)
 
     results = (o_buf, dq_buf, dk_buf, dv_buf)
 
@@ -177,22 +172,16 @@
         each_peer(lambda r: out_copy(i, h, r).start())
         out_own(i, h).start()
 
-    for a in (K, Q, V, G):
-        send_in(a, 0)
-
-    @pl.when(jnp.logical_not(has_left))
+    for h in range(2):
+        for a in (K, V, Q, G):
+            send_in(a, h)
+
+    @pl.when(jnp.logical_not(has_far))
     def _():
-        k_buf[:, 0] = jnp.zeros_like(k_buf[:, 0])
-        v_buf[:, 0] = jnp.zeros_like(v_buf[:, 0])
-        edge_in[:, :, 0] = jnp.zeros_like(edge_in[:, :, 0])
-
-    @pl.when(jnp.logical_not(has_right))
-    def _():
-        k_buf[:, 2] = jnp.zeros_like(k_buf[:, 2])
-        v_buf[:, 2] = jnp.zeros_like(v_buf[:, 2])
-        edge_in[:, :, 1] = jnp.zeros_like(edge_in[:, :, 1])
-
-    seen = (has_left, None, has_right)
+        k_buf[:, FAR] = jnp.zeros_like(k_buf[:, FAR])
+        v_buf[:, FAR] = jnp.zeros_like(v_buf[:, FAR])
+        edge_in[:, :, FAR] = jnp.zeros_like(edge_in[:, :, FAR])
+
     per_slot = block // CHUNK
 
     def piece(c):
@@ -204,13 +193,13 @@
             part = dot(k_buf[h, slot, piece(c)], query_t)
             scores[slot, piece(c)] = part
             best = jnp.maximum(best, jnp.max(part.reshape(CHUNK // 8, 8, block), axis=0))
-        if seen[slot] is not None:
-            best = jnp.where(seen[slot], best, -jnp.inf)
+        if slot == FAR:
+            best = jnp.where(has_far, best, -jnp.inf)
         return best
 
     def slot_weights(h, slot, top):
-        if seen[slot] is not None:
-            top = jnp.where(seen[slot], top, jnp.float32(1e30))
+        if slot == FAR:
+            top = jnp.where(has_far, top, jnp.float32(1e30))
         total = jnp.zeros((8, block), jnp.float32)
         acc = jnp.zeros((HEAD_DIM, block), jnp.float32)
         for c in range(per_slot):
@@ -234,7 +223,8 @@
 
     def finish_keys(h):
         for i, (own, buf, scale) in enumerate(((own_dk, dk_buf, SCALE), (own_dv, dv_buf, 1.0))):
-            wait_recv_pair(edge(i, h))
+            for side in (CORE, FAR):
+                if_there(side, edge(i, h, side).wait_recv)
             total = (
                 own[h]
                 + edge_in[i, h, 0].astype(jnp.float32)
@@ -243,30 +233,27 @@
             buf[h] = (total * scale).astype(jnp.bfloat16)
             send_out(DK + i, h)
 
+    def forward(a, h):
+        wait_in(a, h)
+        start_halo(a, h)
+
+    def wait_halo(a, h, side):
+        if_there(side, halo(a, h, side).wait_recv)
+
+    forward(K, 0)
+    forward(V, 0)
     for h in range(2):
-        if h == 0:
-            wait_in(K, 0)
-            start_pair(halo(K, 0))
-            send_in(K, 1)
         wait_in(Q, h)
         query = q_buf[h]
         query_t = query.T
-        best = slot_scores(h, 1, query_t)
-        if h == 0:
-            wait_in(V, 0)
-            start_pair(halo(V, 0))
-            send_in(Q, 1)
-            send_in(V, 1)
-            send_in(G, 1)
-        wait_recv_pair(halo(K, h))
-        for slot in (0, 2):
+        best = slot_scores(h, OWN, query_t)
+        for slot in (CORE, FAR):
+            wait_halo(K, h, slot)
             best = jnp.maximum(best, slot_scores(h, slot, query_t))
-        if h == 1:
-            finish_keys(0)
-        wait_recv_pair(halo(V, h))
         top = jnp.max(best, axis=0, keepdims=True) * LOG2_SCALE
-        total, acc = slot_weights(h, 1, top)
-        for slot in (0, 2):
+        total, acc = slot_weights(h, OWN, top)
+        for slot in (CORE, FAR):
+            wait_halo(V, h, slot)
             more, term = slot_weights(h, slot, top)
             total, acc = total + more, acc + term
         inverse = 1.0 / jnp.sum(total, axis=0, keepdims=True)
@@ -274,8 +261,9 @@
         o_buf[h] = attended_t.T
         send_out(O, h)
         if h == 0:
-            wait_in(K, 1)
-            start_pair(halo(K, 1))
+            forward(K, 1)
+        else:
+            finish_keys(0)
         wait_in(G, h)
         grad_t = (g_buf[h].T.astype(jnp.float32) * inverse).astype(jnp.bfloat16)
         row_dot = jnp.sum(
@@ -283,27 +271,30 @@
         )
         grad = grad_t.T
         acc = slot_grads(
-            h, 2, query, grad, grad_t, row_dot, edge_out.at[0, h, 0], edge_out.at[1, h, 0]
-        )
+            h, FAR, query, grad, grad_t, row_dot, edge_out.at[0, h, FAR], edge_out.at[1, h, FAR]
+        )
+        if h == 0:
+            forward(V, 1)
+        start_edges(h, FAR)
         acc = acc + slot_grads(
-            h, 0, query, grad, grad_t, row_dot, edge_out.at[0, h, 1], edge_out.at[1, h, 1]
-        )
-        start_pair(edge(0, h))
-        start_pair(edge(1, h))
-        if h == 0:
-            wait_in(V, 1)
-            start_pair(halo(V, 1))
-        acc = acc + slot_grads(h, 1, query, grad, grad_t, row_dot, own_dk.at[h], own_dv.at[h])
+            h, CORE, query, grad, grad_t, row_dot, edge_out.at[0, h, CORE], edge_out.at[1, h, CORE]
+        )
+        start_edges(h, CORE)
+        acc = acc + slot_grads(h, OWN, query, grad, grad_t, row_dot, own_dk.at[h], own_dv.at[h])
         dq_buf[h] = (acc * SCALE).astype(jnp.bfloat16).T
         send_out(DQ, h)
-    finish_keys(1)
-
     for h in range(2):
         for a in range(4):
             each_peer(lambda r: in_copy(a, h, r).wait_send())
-        for i in range(2):
-            wait_send_pair(halo((K, V)[i], h))
-            wait_send_pair(edge(i, h))
+        for side in (FAR, CORE):
+            for a in (K, V):
+                if_there(side, halo(a, h, side).wait_send)
+    finish_keys(1)
+
+    for h in range(2):
+        for side in (FAR, CORE):
+            for i in range(2):
+                if_there(side, edge(i, h, side).wait_send)
         for i in range(4):
             each_peer(lambda r: out_copy(i, h, r).wait())
             out_own(i, h).wait()
@@ -311,13 +302,22 @@
 
 def hand_over(*refs):
     sources, targets, (held, fetched, stored) = refs[:4], refs[4:8], refs[8:]
-    fetch = [pltpu.make_async_copy(sources[i], held.at[i], fetched.at[i]) for i in range(4)]
-    store = [pltpu.make_async_copy(held.at[i], targets[i], stored.at[i]) for i in range(4)]
+    count = fetched.shape[1]
+    rows = held.shape[1] // count
+    pieces = [(i, j, pl.ds(j * rows, rows)) for i in range(4) for j in range(count)]
+    fetch = [
+        pltpu.make_async_copy(sources[i].at[part], held.at[i, part], fetched.at[i, j])
+        for i, j, part in pieces
+    ]
+    store = [
+        pltpu.make_async_copy(held.at[i, part], targets[i].at[part], stored.at[i, j])
+        for i, j, part in pieces
+    ]
     for copy in fetch:
         copy.start()
-    for i in range(4):
-        fetch[i].wait()
-        store[i].start()
+    for before, after in zip(fetch, store):
+        before.wait()
+        after.start()
     for copy in store:
         copy.wait()
 
@@ -373,7 +373,7 @@
         in_specs=[whole] * 4,
         out_specs=[whole] * 4,
         out_shape=[jax.ShapeDtypeStruct(query_in.shape, low)] * 4,
-        scratch_shapes=[pltpu.VMEM((4, *query_in.shape), low), dma((4,)), dma((4,))],
+        scratch_shapes=[pltpu.VMEM((4, *query_in.shape), low), dma((4, 4)), dma((4, 4))],
     )(*results)
 
 

time: 70.5 us -> 62.7 us (0.89)
  Pallas kernels: 69.6 us -> 61.8 us
    pallas_call x1, Pallas kernels: 67.2 us -> 59.3 us  [local(): pl.pallas_call(kernel, in_specs=[whole] * 4, out_specs=[whole] * 4, out_s...]
where the time goes in v3:
time: 62.7 us; the launch traced here: 62.6 us
  Pallas kernels  61.8 us (99%)
  between operations  0.8 us (1%)
    pallas_call x1, Pallas kernels, local(): pl.pallas_call(kernel, in_specs=[whole] * 4, out_specs=[whole] * 4, out_s...  59.3 us
    pallas_call x1, Pallas kernels, local(): pl.pallas_call(hand_over, in_specs=[whole] * 4, out_specs=[whole] * 4, ou...  2.57 us

profile of v3, /device:TPU:16, one launch (start us, length us, event | category | flops | bytes accessed | tf_op | source)
XLA Modules:
  0.0 62.6 jit_solution(12402583447090967480)
XLA Ops:
  0.6 59.3 %shard_map.75 = (bf16[128,2048]{1,0:T(8,128)(2,1)}, bf16[128,2048]{1,0:T(8,128)(2,1)}, bf16[128,2048]{1,0:T(8,128)(2,1)}, bf16[128,2048]{1,0:T(8,128)(2,1)}) custom-call(bf16[128,2048]{1,0:T(8,128)(2,1)} %q_in.1, bf16[128,2048]{1,0:T(8,128)(2,1)} %k_in.1, bf16[128,2048]{1,0:T(8,128)(2,1)} %v_in.1, bf16[128,2048]{1,0:T(8,128)(2,1)} %g_in.1), custom_call_target="tpu_custom_call" | custom-call | flops 9663676416 | bytes 4194304 | tf_op jit(solution)/shard_map/pallas_call | solution.py:333
  59.9 2.6 %shard_map.76 = (bf16[128,2048]{1,0:T(8,128)(2,1)}, bf16[128,2048]{1,0:T(8,128)(2,1)}, bf16[128,2048]{1,0:T(8,128)(2,1)}, bf16[128,2048]{1,0:T(8,128)(2,1)}) custom-call(bf16[128,2048]{1,0:T(8,128)(2,1)} %get-tuple-element.8.refs_0_, bf16[128,2048]{1,0:T(8,128)(2,1)} %get-tuple-element.9.refs_1_, bf16[128,2048]{1,0:T(8,128)(2,1)} %get-tuple-element.10.refs_2_, ...), custom_call_target="tpu_custom_call" | custom-call | tf_op jit(solution)/shard_map/pallas_call | solution.py:371

commit v4 on v3

--- a/solution.py
+++ b/solution.py
@@ -77,33 +77,43 @@
 
     pl.semaphore_wait(barrier, width + has_far.astype(jnp.int32))
 
+    per_slot = block // CHUNK
+
+    def piece(c):
+        return slice(c * CHUNK, (c + 1) * CHUNK)
+
     def columns(owner, h):
         return pl.ds(pl.multiple_of((heads_of(owner) * 2 + h) * HEAD_DIM, HEAD_DIM), HEAD_DIM)
 
     def token_rows(owner):
         return pl.ds(pl.multiple_of(owner * rows, rows), rows)
 
+    def landing(a, h):
+        if a == Q:
+            return q_buf.at[h]
+        if a == G:
+            return g_buf.at[h]
+        return (k_buf if a == K else v_buf).at[h, OWN]
+
     def in_place(a, h):
-        if a == Q:
-            return q_buf.at[h, token_rows(member)]
-        if a == G:
-            return g_buf.at[h, token_rows(member)]
-        buf = k_buf if a == K else v_buf
-        return buf.at[h, OWN, token_rows(member)]
+        return landing(a, h).at[token_rows(member)]
+
+    def wait_bytes(ref, sem):
+        pltpu.make_async_copy(ref, ref, sem).wait()
 
     def in_copy(a, h, r):
         return pltpu.make_async_remote_copy(
             src_ref=inputs[a].at[:, columns(peer(r), h)],
             dst_ref=in_place(a, h),
-            send_sem=in_send.at[a, h, r],
-            recv_sem=in_recv.at[a, h, r],
+            send_sem=in_send.at[a],
+            recv_sem=in_recv.at[a, h],
             device_id=(place, peer(r)),
             device_id_type=MESH,
         )
 
     def in_own(a, h):
         return pltpu.make_async_copy(
-            inputs[a].at[:, columns(member, h)], in_place(a, h), in_recv.at[a, h, 0]
+            inputs[a].at[:, columns(member, h)], in_place(a, h), in_recv.at[a, h]
         )
 
     def send_in(a, h):
@@ -111,25 +121,24 @@
         in_own(a, h).start()
 
     def wait_in(a, h):
-        each_peer(lambda r: in_copy(a, h, r).wait_recv())
-        in_own(a, h).wait()
+        wait_bytes(landing(a, h), in_recv.at[a, h])
 
     def halo(a, h, side):
         buf, i = (k_buf, 0) if a == K else (v_buf, 1)
         return pltpu.make_async_remote_copy(
             src_ref=buf.at[h, OWN],
             dst_ref=buf.at[h, side],
-            send_sem=halo_send.at[i, h, side],
+            send_sem=halo_send.at[i, side],
             recv_sem=halo_recv.at[i, h, side],
             device_id=sides[side],
             device_id_type=MESH,
         )
 
-    def edge(i, h, side):
+    def edge(i, h, side, c):
         return pltpu.make_async_remote_copy(
-            src_ref=edge_out.at[i, h, side],
-            dst_ref=edge_in.at[i, h, side],
-            send_sem=edge_send.at[i, h, side],
+            src_ref=edge_out.at[i, h, side, pl.ds(c * CHUNK, CHUNK)],
+            dst_ref=edge_in.at[i, h, side, pl.ds(c * CHUNK, CHUNK)],
+            send_sem=edge_send.at[i, side],
             recv_sem=edge_recv.at[i, h, side],
             device_id=sides[side],
             device_id_type=MESH,
@@ -145,18 +154,14 @@
         for side in (FAR, CORE):
             if_there(side, halo(a, h, side).start)
 
-    def start_edges(h, side):
-        for i in range(2):
-            if_there(side, edge(i, h, side).start)
-
     results = (o_buf, dq_buf, dk_buf, dv_buf)
 
     def out_copy(i, h, r):
         return pltpu.make_async_remote_copy(
             src_ref=results[i].at[h, token_rows(peer(r))],
             dst_ref=outputs[i].at[:, columns(member, h)],
-            send_sem=out_send.at[i, h, r],
-            recv_sem=out_recv.at[i, h, r],
+            send_sem=out_send.at[i],
+            recv_sem=out_recv.at[i],
             device_id=(place, peer(r)),
             device_id_type=MESH,
         )
@@ -165,27 +170,21 @@
         return pltpu.make_async_copy(
             results[i].at[h, token_rows(member)],
             outputs[i].at[:, columns(member, h)],
-            out_recv.at[i, h, 0],
+            out_recv.at[i],
         )
 
     def send_out(i, h):
         each_peer(lambda r: out_copy(i, h, r).start())
         out_own(i, h).start()
 
-    for h in range(2):
-        for a in (K, V, Q, G):
-            send_in(a, h)
+    for a, h in ((K, 0), (V, 0), (Q, 0), (K, 1), (G, 0), (V, 1), (Q, 1), (G, 1)):
+        send_in(a, h)
 
     @pl.when(jnp.logical_not(has_far))
     def _():
         k_buf[:, FAR] = jnp.zeros_like(k_buf[:, FAR])
         v_buf[:, FAR] = jnp.zeros_like(v_buf[:, FAR])
         edge_in[:, :, FAR] = jnp.zeros_like(edge_in[:, :, FAR])
-
-    per_slot = block // CHUNK
-
-    def piece(c):
-        return slice(c * CHUNK, (c + 1) * CHUNK)
 
     def slot_scores(h, slot, query_t):
         best = jnp.full((8, block), -jnp.inf, jnp.float32)
@@ -218,13 +217,18 @@
             grad_scores = (low.astype(jnp.float32) * (grad_probs - row_dot)).astype(jnp.bfloat16)
             dv_ref[piece(c)] = dot(low, grad).astype(dv_ref.dtype)
             dk_ref[piece(c)] = dot(grad_scores, query).astype(dk_ref.dtype)
+            if slot != OWN:
+                for i in range(2):
+                    if_there(slot, edge(i, h, slot, c).start)
             acc = acc + dot(k_buf[h, slot, piece(c)].T, grad_scores)
         return acc
 
     def finish_keys(h):
         for i, (own, buf, scale) in enumerate(((own_dk, dk_buf, SCALE), (own_dv, dv_buf, 1.0))):
             for side in (CORE, FAR):
-                if_there(side, edge(i, h, side).wait_recv)
+                if_there(
+                    side, lambda: wait_bytes(edge_in.at[i, h, side], edge_recv.at[i, h, side])
+                )
             total = (
                 own[h]
                 + edge_in[i, h, 0].astype(jnp.float32)
@@ -253,6 +257,8 @@
         top = jnp.max(best, axis=0, keepdims=True) * LOG2_SCALE
         total, acc = slot_weights(h, OWN, top)
         for slot in (CORE, FAR):
+            if h == 0 and slot == FAR:
+                forward(K, 1)
             wait_halo(V, h, slot)
             more, term = slot_weights(h, slot, top)
             total, acc = total + more, acc + term
@@ -260,65 +266,59 @@
         attended_t = (acc * inverse).astype(jnp.bfloat16)
         o_buf[h] = attended_t.T
         send_out(O, h)
-        if h == 0:
-            forward(K, 1)
-        else:
-            finish_keys(0)
         wait_in(G, h)
         grad_t = (g_buf[h].T.astype(jnp.float32) * inverse).astype(jnp.bfloat16)
         row_dot = jnp.sum(
             grad_t.astype(jnp.float32) * attended_t.astype(jnp.float32), axis=0, keepdims=True
         )
         grad = grad_t.T
-        acc = slot_grads(
-            h, FAR, query, grad, grad_t, row_dot, edge_out.at[0, h, FAR], edge_out.at[1, h, FAR]
-        )
-        if h == 0:
-            forward(V, 1)
-        start_edges(h, FAR)
-        acc = acc + slot_grads(
-            h, CORE, query, grad, grad_t, row_dot, edge_out.at[0, h, CORE], edge_out.at[1, h, CORE]
-        )
-        start_edges(h, CORE)
+        acc = None
+        for slot in (CORE, FAR) if h == 0 else (FAR, CORE):
+            term = slot_grads(
+                h, slot, query, grad, grad_t, row_dot, edge_out.at[0, h, slot], edge_out.at[1, h, slot]
+            )
+            if acc is None:
+                acc = term
+                if h == 0:
+                    forward(V, 1)
+                else:
+                    finish_keys(0)
+            else:
+                acc = acc + term
         acc = acc + slot_grads(h, OWN, query, grad, grad_t, row_dot, own_dk.at[h], own_dv.at[h])
         dq_buf[h] = (acc * SCALE).astype(jnp.bfloat16).T
         send_out(DQ, h)
-    for h in range(2):
-        for a in range(4):
-            each_peer(lambda r: in_copy(a, h, r).wait_send())
+    others = pl.ds(0, (width - 1) * rows)
+    for a, buf in ((Q, q_buf), (G, g_buf)):
+        wait_bytes(buf.at[:, others], in_send.at[a])
+    for i, buf in enumerate((k_buf, v_buf)):
+        wait_bytes(buf.at[:, OWN, others], in_send.at[(K, V)[i]])
         for side in (FAR, CORE):
-            for a in (K, V):
-                if_there(side, halo(a, h, side).wait_send)
+            if_there(side, lambda: wait_bytes(buf.at[:, side], halo_send.at[i, side]))
     finish_keys(1)
 
-    for h in range(2):
+    for i in range(2):
         for side in (FAR, CORE):
-            for i in range(2):
-                if_there(side, edge(i, h, side).wait_send)
-        for i in range(4):
-            each_peer(lambda r: out_copy(i, h, r).wait())
-            out_own(i, h).wait()
+            if_there(side, lambda: wait_bytes(edge_out.at[i, :, side], edge_send.at[i, side]))
+    for i in range(4):
+        wait_bytes(results[i].at[:, others], out_send.at[i])
+        wait_bytes(outputs[i], out_recv.at[i])
 
 
 def hand_over(*refs):
-    sources, targets, (held, fetched, stored) = refs[:4], refs[4:8], refs[8:]
-    count = fetched.shape[1]
-    rows = held.shape[1] // count
-    pieces = [(i, j, pl.ds(j * rows, rows)) for i in range(4) for j in range(count)]
-    fetch = [
-        pltpu.make_async_copy(sources[i].at[part], held.at[i, part], fetched.at[i, j])
-        for i, j, part in pieces
+    sources, targets, done = refs[:4], refs[4:8], refs[8]
+    count = done.shape[1]
+    rows = sources[0].shape[0] // count
+    copies = [
+        pltpu.make_async_copy(
+            sources[i].at[pl.ds(j * rows, rows)], targets[i].at[pl.ds(j * rows, rows)], done.at[i, j]
+        )
+        for i in range(4)
+        for j in range(count)
     ]
-    store = [
-        pltpu.make_async_copy(held.at[i, part], targets[i].at[part], stored.at[i, j])
-        for i, j, part in pieces
-    ]
-    for copy in fetch:
+    for copy in copies:
         copy.start()
-    for before, after in zip(fetch, store):
-        before.wait()
-        after.start()
-    for copy in store:
+    for copy in copies:
         copy.wait()
 
 
@@ -330,11 +330,15 @@
     low, full = jnp.bfloat16, jnp.float32
     dma = pltpu.SemaphoreType.DMA
     whole = pl.BlockSpec(memory_space=pl.ANY)
+    query_in, key_in, value_in, out_grad = (
+        pltpu.with_memory_space_constraint(array, pltpu.HBM)
+        for array in (query_in, key_in, value_in, out_grad)
+    )
     results = pl.pallas_call(
         kernel,
         in_specs=[whole] * 4,
         out_specs=[whole] * 4,
-        out_shape=[jax.ShapeDtypeStruct(query_in.shape, low)] * 4,
+        out_shape=[pltpu.VMEM(query_in.shape, low)] * 4,
         scratch_shapes=[
             pltpu.VMEM((heads, block, HEAD_DIM), low),
             pltpu.VMEM((heads, block, HEAD_DIM), low),
@@ -350,17 +354,17 @@
             pltpu.VMEM((heads, block, HEAD_DIM), full),
             pltpu.VMEM((2, heads, 2, block, HEAD_DIM), low),
             pltpu.VMEM((2, heads, 2, block, HEAD_DIM), low),
-            dma((4, heads, width)),
-            dma((4, heads, width)),
+            dma((4,)),
+            dma((4, heads)),
+            dma((2, 2)),
             dma((2, heads, 2)),
+            dma((2, 2)),
             dma((2, heads, 2)),
-            dma((2, heads, 2)),
-            dma((2, heads, 2)),
-            dma((4, heads, width)),
-            dma((4, heads, width)),
+            dma((4,)),
+            dma((4,)),
         ],
         compiler_params=pltpu.CompilerParams(
-            collective_id=0, has_side_effects=True, vmem_limit_bytes=60 * 2**20
+            collective_id=0, has_side_effects=True, vmem_limit_bytes=44 * 2**20
         ),
         cost_estimate=pl.CostEstimate(
             flops=12 * heads * 3 * block * block * HEAD_DIM,
@@ -373,8 +377,8 @@
         in_specs=[whole] * 4,
         out_specs=[whole] * 4,
         out_shape=[jax.ShapeDtypeStruct(query_in.shape, low)] * 4,
-        scratch_shapes=[pltpu.VMEM((4, *query_in.shape), low), dma((4, 4)), dma((4, 4))],
-    )(*results)
+        scratch_shapes=[dma((4, 4))],
+    )(*(pltpu.with_memory_space_constraint(result, pltpu.VMEM) for result in results))
 
 
 def solution(mesh):

time: 62.7 us -> 57.8 us (0.922)
  Pallas kernels: 61.8 us -> 56.6 us
    pallas_call x1, Pallas kernels: 59.3 us -> 55.1 us  [local(): pl.pallas_call(kernel, in_specs=[whole] * 4, out_specs=[whole] * 4, out_s...]
    pallas_call x1, Pallas kernels: 2.57 us -> 1.44 us  [local(): pl.pallas_call(hand_over, in_specs=[whole] * 4, out_specs=[whole] * 4, ou...]
where the time goes in v4:
time: 57.8 us; the launch traced here: 57.4 us
  Pallas kernels  56.6 us (98%)
  between operations  0.82 us (1%)
    pallas_call x1, Pallas kernels, local(): pl.pallas_call(kernel, in_specs=[whole] * 4, out_specs=[whole] * 4, out_s...  55.1 us
    pallas_call x1, Pallas kernels, local(): pl.pallas_call(hand_over, in_specs=[whole] * 4, out_specs=[whole] * 4, ou...  1.44 us

profile of v4, /device:TPU:16, one launch (start us, length us, event | category | flops | bytes accessed | tf_op | source)
XLA Modules:
  0.0 57.4 jit_solution(14386680267208134680)
XLA Ops:
  0.6 55.1 %shard_map.75 = (bf16[128,2048]{1,0:T(8,128)(2,1)S(1)}, bf16[128,2048]{1,0:T(8,128)(2,1)S(1)}, bf16[128,2048]{1,0:T(8,128)(2,1)S(1)}, bf16[128,2048]{1,0:T(8,128)(2,1)S(1)}) custom-call(bf16[128,2048]{1,0:T(8,128)(2,1)} %q_in.1, bf16[128,2048]{1,0:T(8,128)(2,1)} %k_in.1, bf16[128,2048]{1,0:T(8,128)(2,1)} %v_in.1, bf16[128,2048]{1,0:T(8,128)(2,1)} %g_in.1), custom_call_target="tpu_custom_call" | custom-call | flops 9663676416 | bytes 4194304 | tf_op jit(solution)/shard_map/pallas_call | solution.py:337
  55.7 1.4 %shard_map.76 = (bf16[128,2048]{1,0:T(8,128)(2,1)}, bf16[128,2048]{1,0:T(8,128)(2,1)}, bf16[128,2048]{1,0:T(8,128)(2,1)}, bf16[128,2048]{1,0:T(8,128)(2,1)}) custom-call(bf16[128,2048]{1,0:T(8,128)(2,1)S(1)} %get-tuple-element.8.refs_0_, bf16[128,2048]{1,0:T(8,128)(2,1)S(1)} %get-tuple-element.9.refs_1_, bf16[128,2048]{1,0:T(8,128)(2,1)S(1)} %get-tuple-element.10.refs_2_, ...), custom_call_target="tpu_custom_call" | custom-call | tf_op jit(solution)/shard_map/pallas_call | solution.py:375

commit v5 on v4

--- a/solution.py
+++ b/solution.py
@@ -14,6 +14,7 @@
 Q, K, V, G = range(4)
 O, DQ, DK, DV = range(4)
 FAR, CORE, OWN = range(3)
+FAR_FIRST = 0o6214735
 
 
 def dot(a, b):
@@ -24,7 +25,7 @@
     q_in, k_in, v_in, g_in, o_out, dq_out, dk_out, dv_out,
     q_buf, g_buf, k_buf, v_buf, scores, weights, o_buf, dq_buf, dk_buf, dv_buf,
     own_dk, own_dv, edge_out, edge_in,
-    in_send, in_recv, halo_send, halo_recv, edge_send, edge_recv, out_send, out_recv,
+    in_send, in_recv, halo_send, halo_recv, edge_send, edge_recv, out_send, out_recv, near,
 ):
     rows = q_in.shape[0]
     block = q_buf.shape[1]
@@ -61,7 +62,9 @@
     )
 
     def each_peer(body):
-        lax.fori_loop(1, width, lambda r, _: (body(jnp.int32(r)), 0)[1], 0)
+        lax.fori_loop(
+            1, width, lambda _, code: (body(lax.rem(code, 8)), lax.div(code, 8))[1], jnp.int32(FAR_FIRST)
+        )
 
     barrier = pltpu.get_barrier_semaphore()
     each_peer(
@@ -71,11 +74,20 @@
     )
     pl.semaphore_signal(barrier, inc=1, device_id=sides[CORE], device_id_type=MESH)
 
-    @pl.when(has_far)
+    spot, middle = lax.rem(place, blocks // 2), blocks // 4
+    waits = jnp.logical_or(jnp.logical_and(core == 1, spot != middle - 1), spot == middle)
+    greets_far = jnp.logical_and(has_far, jnp.logical_not(waits))
+    waits_far = jnp.logical_and(has_far, waits)
+
+    @pl.when(greets_far)
     def _():
         pl.semaphore_signal(barrier, inc=1, device_id=sides[FAR], device_id_type=MESH)
 
-    pl.semaphore_wait(barrier, width + has_far.astype(jnp.int32))
+    pl.semaphore_wait(barrier, width + waits_far.astype(jnp.int32))
+
+    @pl.when(waits_far)
+    def _():
+        pl.semaphore_signal(near, inc=1, device_id=sides[FAR], device_id_type=MESH)
 
     per_slot = block // CHUNK
 
@@ -243,6 +255,10 @@
 
     def wait_halo(a, h, side):
         if_there(side, halo(a, h, side).wait_recv)
+
+    @pl.when(greets_far)
+    def _():
+        pl.semaphore_wait(near, 1)
 
     forward(K, 0)
     forward(V, 0)
@@ -362,6 +378,7 @@
             dma((2, heads, 2)),
             dma((4,)),
             dma((4,)),
+            pltpu.SemaphoreType.REGULAR,
         ],
         compiler_params=pltpu.CompilerParams(
             collective_id=0, has_side_effects=True, vmem_limit_bytes=44 * 2**20
@@ -377,7 +394,7 @@
         in_specs=[whole] * 4,
         out_specs=[whole] * 4,
         out_shape=[jax.ShapeDtypeStruct(query_in.shape, low)] * 4,
-        scratch_shapes=[dma((4, 4))],
+        scratch_shapes=[dma((4, 1))],
     )(*(pltpu.with_memory_space_constraint(result, pltpu.VMEM) for result in results))
 
 

time: 57.8 us -> 56.1 us (0.971)
  Pallas kernels: 56.6 us -> 54.7 us
    pallas_call x1, Pallas kernels: 55.1 us -> 53.4 us  [local(): pl.pallas_call(kernel, in_specs=[whole] * 4, out_specs=[whole] * 4, out_s...]
where the time goes in v5:
time: 56.1 us; the launch traced here: 55.5 us
  Pallas kernels  54.7 us (98%)
  between operations  0.82 us (1%)
    pallas_call x1, Pallas kernels, local(): pl.pallas_call(kernel, in_specs=[whole] * 4, out_specs=[whole] * 4, out_s...  53.4 us
    pallas_call x1, Pallas kernels, local(): pl.pallas_call(hand_over, in_specs=[whole] * 4, out_specs=[whole] * 4, ou...  1.35 us

profile of v5, /device:TPU:16, one launch (start us, length us, event | category | flops | bytes accessed | tf_op | source)
XLA Modules:
  0.0 55.5 jit_solution(1537731387250023641)
XLA Ops:
  0.6 53.4 %shard_map.75 = (bf16[128,2048]{1,0:T(8,128)(2,1)S(1)}, bf16[128,2048]{1,0:T(8,128)(2,1)S(1)}, bf16[128,2048]{1,0:T(8,128)(2,1)S(1)}, bf16[128,2048]{1,0:T(8,128)(2,1)S(1)}) custom-call(bf16[128,2048]{1,0:T(8,128)(2,1)} %q_in.1, bf16[128,2048]{1,0:T(8,128)(2,1)} %k_in.1, bf16[128,2048]{1,0:T(8,128)(2,1)} %v_in.1, bf16[128,2048]{1,0:T(8,128)(2,1)} %g_in.1), custom_call_target="tpu_custom_call" | custom-call | flops 9663676416 | bytes 4194304 | tf_op jit(solution)/shard_map/pallas_call | solution.py:353
  54.0 1.3 %shard_map.76 = (bf16[128,2048]{1,0:T(8,128)(2,1)}, bf16[128,2048]{1,0:T(8,128)(2,1)}, bf16[128,2048]{1,0:T(8,128)(2,1)}, bf16[128,2048]{1,0:T(8,128)(2,1)}) custom-call(bf16[128,2048]{1,0:T(8,128)(2,1)S(1)} %get-tuple-element.8.refs_0_, bf16[128,2048]{1,0:T(8,128)(2,1)S(1)} %get-tuple-element.9.refs_1_, bf16[128,2048]{1,0:T(8,128)(2,1)S(1)} %get-tuple-element.10.refs_2_, ...), custom_call_target="tpu_custom_call" | custom-call | tf_op jit(solution)/shard_map/pallas_call | solution.py:392

commit v6 on v5

--- a/solution.py
+++ b/solution.py
@@ -25,7 +25,7 @@
     q_in, k_in, v_in, g_in, o_out, dq_out, dk_out, dv_out,
     q_buf, g_buf, k_buf, v_buf, scores, weights, o_buf, dq_buf, dk_buf, dv_buf,
     own_dk, own_dv, edge_out, edge_in,
-    in_send, in_recv, halo_send, halo_recv, edge_send, edge_recv, out_send, out_recv, near,
+    in_send, in_recv, first_recv, halo_send, halo_recv, edge_send, edge_recv, out_send, out_recv, near,
 ):
     rows = q_in.shape[0]
     block = q_buf.shape[1]
@@ -42,6 +42,11 @@
         y = lax.rem(column_y + lax.rem(r, 2), 2)
         return x * 2 + y
 
+    def source(r):
+        x = lax.rem(column_x + width // 2 - lax.div(r, 2), width // 2)
+        y = lax.rem(column_y + lax.rem(r, 2), 2)
+        return x * 2 + y
+
     def flipped(owner):
         return owner + 1 - 2 * lax.rem(owner, 2)
 
@@ -66,28 +71,23 @@
             1, width, lambda _, code: (body(lax.rem(code, 8)), lax.div(code, 8))[1], jnp.int32(FAR_FIRST)
         )
 
-    barrier = pltpu.get_barrier_semaphore()
-    each_peer(
-        lambda r: pl.semaphore_signal(
-            barrier, inc=1, device_id=(place, peer(r)), device_id_type=MESH
-        )
-    )
-    pl.semaphore_signal(barrier, inc=1, device_id=sides[CORE], device_id_type=MESH)
-
     spot, middle = lax.rem(place, blocks // 2), blocks // 4
     waits = jnp.logical_or(jnp.logical_and(core == 1, spot != middle - 1), spot == middle)
     greets_far = jnp.logical_and(has_far, jnp.logical_not(waits))
     waits_far = jnp.logical_and(has_far, waits)
 
+    barrier = pltpu.get_barrier_semaphore()
+
     @pl.when(greets_far)
     def _():
         pl.semaphore_signal(barrier, inc=1, device_id=sides[FAR], device_id_type=MESH)
 
-    pl.semaphore_wait(barrier, width + waits_far.astype(jnp.int32))
-
-    @pl.when(waits_far)
-    def _():
-        pl.semaphore_signal(near, inc=1, device_id=sides[FAR], device_id_type=MESH)
+    each_peer(
+        lambda r: pl.semaphore_signal(
+            barrier, inc=1, device_id=(place, peer(r)), device_id_type=MESH
+        )
+    )
+    pl.semaphore_signal(barrier, inc=1, device_id=sides[CORE], device_id_type=MESH)
 
     per_slot = block // CHUNK
 
@@ -107,6 +107,9 @@
             return g_buf.at[h]
         return (k_buf if a == K else v_buf).at[h, OWN]
 
+    def arrived(a, h, r):
+        return first_recv.at[(K, V).index(a), r] if h == 0 and a in (K, V) else in_recv.at[a, h]
+
     def in_place(a, h):
         return landing(a, h).at[token_rows(member)]
 
@@ -118,28 +121,27 @@
             src_ref=inputs[a].at[:, columns(peer(r), h)],
             dst_ref=in_place(a, h),
             send_sem=in_send.at[a],
-            recv_sem=in_recv.at[a, h],
+            recv_sem=arrived(a, h, r),
             device_id=(place, peer(r)),
             device_id_type=MESH,
         )
 
     def in_own(a, h):
         return pltpu.make_async_copy(
-            inputs[a].at[:, columns(member, h)], in_place(a, h), in_recv.at[a, h]
+            inputs[a].at[:, columns(member, h)], in_place(a, h), arrived(a, h, 0)
         )
 
     def send_in(a, h):
         each_peer(lambda r: in_copy(a, h, r).start())
-        in_own(a, h).start()
 
     def wait_in(a, h):
         wait_bytes(landing(a, h), in_recv.at[a, h])
 
-    def halo(a, h, side):
+    def halo(a, h, side, part=slice(None)):
         buf, i = (k_buf, 0) if a == K else (v_buf, 1)
         return pltpu.make_async_remote_copy(
-            src_ref=buf.at[h, OWN],
-            dst_ref=buf.at[h, side],
+            src_ref=buf.at[h, OWN, part],
+            dst_ref=buf.at[h, side, part],
             send_sem=halo_send.at[i, side],
             recv_sem=halo_recv.at[i, h, side],
             device_id=sides[side],
@@ -189,7 +191,17 @@
         each_peer(lambda r: out_copy(i, h, r).start())
         out_own(i, h).start()
 
-    for a, h in ((K, 0), (V, 0), (Q, 0), (K, 1), (G, 0), (V, 1), (Q, 1), (G, 1)):
+    order = ((K, 0), (V, 0), (Q, 0), (K, 1), (G, 0), (V, 1), (Q, 1), (G, 1))
+    for a, h in order:
+        in_own(a, h).start()
+
+    pl.semaphore_wait(barrier, width + waits_far.astype(jnp.int32))
+
+    @pl.when(waits_far)
+    def _():
+        pl.semaphore_signal(near, inc=1, device_id=sides[FAR], device_id_type=MESH)
+
+    for a, h in order:
         send_in(a, h)
 
     @pl.when(jnp.logical_not(has_far))
@@ -253,6 +265,16 @@
         wait_in(a, h)
         start_halo(a, h)
 
+    def forward_pieces(a):
+        def step(r):
+            part = token_rows(source(r))
+            wait_bytes(landing(a, 0).at[part], arrived(a, 0, r))
+            for side in (FAR, CORE):
+                if_there(side, halo(a, 0, side, part).start)
+
+        step(jnp.int32(0))
+        each_peer(step)
+
     def wait_halo(a, h, side):
         if_there(side, halo(a, h, side).wait_recv)
 
@@ -260,8 +282,8 @@
     def _():
         pl.semaphore_wait(near, 1)
 
-    forward(K, 0)
-    forward(V, 0)
+    forward_pieces(K)
+    forward_pieces(V)
     for h in range(2):
         wait_in(Q, h)
         query = q_buf[h]
@@ -372,6 +394,7 @@
             pltpu.VMEM((2, heads, 2, block, HEAD_DIM), low),
             dma((4,)),
             dma((4, heads)),
+            dma((2, width)),
             dma((2, 2)),
             dma((2, heads, 2)),
             dma((2, 2)),

time: 56.1 us -> 55.8 us (level)
  no operation moved by 1% of the time
where the time goes in v6:
time: 55.8 us; the launch traced here: 55.3 us
  Pallas kernels  54.5 us (98%)
  between operations  0.8 us (1%)
    pallas_call x1, Pallas kernels, local(): pl.pallas_call(kernel, in_specs=[whole] * 4, out_specs=[whole] * 4, out_s...  53.1 us
    pallas_call x1, Pallas kernels, local(): pl.pallas_call(hand_over, in_specs=[whole] * 4, out_specs=[whole] * 4, ou...  1.35 us

profile of v6, /device:TPU:16, one launch (start us, length us, event | category | flops | bytes accessed | tf_op | source)
XLA Modules:
  0.0 55.3 jit_solution(4129613661789864176)
XLA Ops:
  0.6 53.1 %shard_map.75 = (bf16[128,2048]{1,0:T(8,128)(2,1)S(1)}, bf16[128,2048]{1,0:T(8,128)(2,1)S(1)}, bf16[128,2048]{1,0:T(8,128)(2,1)S(1)}, bf16[128,2048]{1,0:T(8,128)(2,1)S(1)}) custom-call(bf16[128,2048]{1,0:T(8,128)(2,1)} %q_in.1, bf16[128,2048]{1,0:T(8,128)(2,1)} %k_in.1, bf16[128,2048]{1,0:T(8,128)(2,1)} %v_in.1, bf16[128,2048]{1,0:T(8,128)(2,1)} %g_in.1), custom_call_target="tpu_custom_call" | custom-call | flops 9663676416 | bytes 4194304 | tf_op jit(solution)/shard_map/pallas_call | solution.py:375
  53.8 1.3 %shard_map.76 = (bf16[128,2048]{1,0:T(8,128)(2,1)}, bf16[128,2048]{1,0:T(8,128)(2,1)}, bf16[128,2048]{1,0:T(8,128)(2,1)}, bf16[128,2048]{1,0:T(8,128)(2,1)}) custom-call(bf16[128,2048]{1,0:T(8,128)(2,1)S(1)} %get-tuple-element.8.refs_0_, bf16[128,2048]{1,0:T(8,128)(2,1)S(1)} %get-tuple-element.9.refs_1_, bf16[128,2048]{1,0:T(8,128)(2,1)S(1)} %get-tuple-element.10.refs_2_, ...), custom_call_target="tpu_custom_call" | custom-call | tf_op jit(solution)/shard_map/pallas_call | solution.py:415

commit v7 on v6

--- a/solution.py
+++ b/solution.py
@@ -120,7 +120,7 @@
         return pltpu.make_async_remote_copy(
             src_ref=inputs[a].at[:, columns(peer(r), h)],
             dst_ref=in_place(a, h),
-            send_sem=in_send.at[a],
+            send_sem=in_send.at[0],
             recv_sem=arrived(a, h, r),
             device_id=(place, peer(r)),
             device_id_type=MESH,
@@ -142,17 +142,17 @@
         return pltpu.make_async_remote_copy(
             src_ref=buf.at[h, OWN, part],
             dst_ref=buf.at[h, side, part],
-            send_sem=halo_send.at[i, side],
+            send_sem=halo_send.at[side],
             recv_sem=halo_recv.at[i, h, side],
             device_id=sides[side],
             device_id_type=MESH,
         )
 
-    def edge(i, h, side, c):
+    def edge(i, h, side):
         return pltpu.make_async_remote_copy(
-            src_ref=edge_out.at[i, h, side, pl.ds(c * CHUNK, CHUNK)],
-            dst_ref=edge_in.at[i, h, side, pl.ds(c * CHUNK, CHUNK)],
-            send_sem=edge_send.at[i, side],
+            src_ref=edge_out.at[i, h, side],
+            dst_ref=edge_in.at[i, h, side],
+            send_sem=edge_send.at[side],
             recv_sem=edge_recv.at[i, h, side],
             device_id=sides[side],
             device_id_type=MESH,
@@ -174,7 +174,7 @@
         return pltpu.make_async_remote_copy(
             src_ref=results[i].at[h, token_rows(peer(r))],
             dst_ref=outputs[i].at[:, columns(member, h)],
-            send_sem=out_send.at[i],
+            send_sem=out_send.at[0],
             recv_sem=out_recv.at[i],
             device_id=(place, peer(r)),
             device_id_type=MESH,
@@ -241,10 +241,10 @@
             grad_scores = (low.astype(jnp.float32) * (grad_probs - row_dot)).astype(jnp.bfloat16)
             dv_ref[piece(c)] = dot(low, grad).astype(dv_ref.dtype)
             dk_ref[piece(c)] = dot(grad_scores, query).astype(dk_ref.dtype)
-            if slot != OWN:
-                for i in range(2):
-                    if_there(slot, edge(i, h, slot, c).start)
             acc = acc + dot(k_buf[h, slot, piece(c)].T, grad_scores)
+        if slot != OWN:
+            for i in range(2):
+                if_there(slot, edge(i, h, slot).start)
         return acc
 
     def finish_keys(h):
@@ -326,20 +326,16 @@
         acc = acc + slot_grads(h, OWN, query, grad, grad_t, row_dot, own_dk.at[h], own_dv.at[h])
         dq_buf[h] = (acc * SCALE).astype(jnp.bfloat16).T
         send_out(DQ, h)
-    others = pl.ds(0, (width - 1) * rows)
-    for a, buf in ((Q, q_buf), (G, g_buf)):
-        wait_bytes(buf.at[:, others], in_send.at[a])
-    for i, buf in enumerate((k_buf, v_buf)):
-        wait_bytes(buf.at[:, OWN, others], in_send.at[(K, V)[i]])
-        for side in (FAR, CORE):
-            if_there(side, lambda: wait_bytes(buf.at[:, side], halo_send.at[i, side]))
+    one_side, to_others = edge_out.at[:, :, 0], edge_out.at[:, :, :, pl.ds(0, (width - 1) * rows)]
+    wait_bytes(to_others, in_send.at[0])
+    for side in (FAR, CORE):
+        if_there(side, lambda: wait_bytes(one_side, halo_send.at[side]))
     finish_keys(1)
 
-    for i in range(2):
-        for side in (FAR, CORE):
-            if_there(side, lambda: wait_bytes(edge_out.at[i, :, side], edge_send.at[i, side]))
+    for side in (FAR, CORE):
+        if_there(side, lambda: wait_bytes(one_side, edge_send.at[side]))
+    wait_bytes(to_others, out_send.at[0])
     for i in range(4):
-        wait_bytes(results[i].at[:, others], out_send.at[i])
         wait_bytes(outputs[i], out_recv.at[i])
 
 
@@ -392,14 +388,14 @@
             pltpu.VMEM((heads, block, HEAD_DIM), full),
             pltpu.VMEM((2, heads, 2, block, HEAD_DIM), low),
             pltpu.VMEM((2, heads, 2, block, HEAD_DIM), low),
-            dma((4,)),
+            dma((1,)),
             dma((4, heads)),
             dma((2, width)),
-            dma((2, 2)),
+            dma((2,)),
             dma((2, heads, 2)),
-            dma((2, 2)),
+            dma((2,)),
             dma((2, heads, 2)),
-            dma((4,)),
+            dma((1,)),
             dma((4,)),
             pltpu.SemaphoreType.REGULAR,
         ],

time: 55.8 us -> 55.5 us (level)
  no operation moved by 1% of the time
where the time goes in v7:
time: 55.5 us; the launch traced here: 54.8 us
  Pallas kernels  54 us (97%)
  between operations  0.8 us (1%)
    pallas_call x1, Pallas kernels, local(): pl.pallas_call(kernel, in_specs=[whole] * 4, out_specs=[whole] * 4, out_s...  52.6 us
    pallas_call x1, Pallas kernels, local(): pl.pallas_call(hand_over, in_specs=[whole] * 4, out_specs=[whole] * 4, ou...  1.35 us

profile of v7, /device:TPU:16, one launch (start us, length us, event | category | flops | bytes accessed | tf_op | source)
XLA Modules:
  0.0 54.8 jit_solution(14919178812128573275)
XLA Ops:
  0.6 52.6 %shard_map.75 = (bf16[128,2048]{1,0:T(8,128)(2,1)S(1)}, bf16[128,2048]{1,0:T(8,128)(2,1)S(1)}, bf16[128,2048]{1,0:T(8,128)(2,1)S(1)}, bf16[128,2048]{1,0:T(8,128)(2,1)S(1)}) custom-call(bf16[128,2048]{1,0:T(8,128)(2,1)} %q_in.1, bf16[128,2048]{1,0:T(8,128)(2,1)} %k_in.1, bf16[128,2048]{1,0:T(8,128)(2,1)} %v_in.1, bf16[128,2048]{1,0:T(8,128)(2,1)} %g_in.1), custom_call_target="tpu_custom_call" | custom-call | flops 9663676416 | bytes 4194304 | tf_op jit(solution)/shard_map/pallas_call | solution.py:371
  53.3 1.3 %shard_map.76 = (bf16[128,2048]{1,0:T(8,128)(2,1)}, bf16[128,2048]{1,0:T(8,128)(2,1)}, bf16[128,2048]{1,0:T(8,128)(2,1)}, bf16[128,2048]{1,0:T(8,128)(2,1)}) custom-call(bf16[128,2048]{1,0:T(8,128)(2,1)S(1)} %get-tuple-element.8.refs_0_, bf16[128,2048]{1,0:T(8,128)(2,1)S(1)} %get-tuple-element.9.refs_1_, bf16[128,2048]{1,0:T(8,128)(2,1)S(1)} %get-tuple-element.10.refs_2_, ...), custom_call_target="tpu_custom_call" | custom-call | tf_op jit(solution)/shard_map/pallas_call | solution.py:411

commit v8 on v7

--- a/solution.py
+++ b/solution.py
@@ -11,6 +11,7 @@
 LOG2_SCALE = SCALE * 1.4426950408889634
 MESH = pl.DeviceIdType.MESH
 CHUNK = 512
+SCORE_CHUNK = 256
 Q, K, V, G = range(4)
 O, DQ, DK, DV = range(4)
 FAR, CORE, OWN = range(3)
@@ -210,12 +211,15 @@
         v_buf[:, FAR] = jnp.zeros_like(v_buf[:, FAR])
         edge_in[:, :, FAR] = jnp.zeros_like(edge_in[:, :, FAR])
 
+    def score_piece(c):
+        return slice(c * SCORE_CHUNK, (c + 1) * SCORE_CHUNK)
+
     def slot_scores(h, slot, query_t):
         best = jnp.full((8, block), -jnp.inf, jnp.float32)
-        for c in range(per_slot):
-            part = dot(k_buf[h, slot, piece(c)], query_t)
-            scores[slot, piece(c)] = part
-            best = jnp.maximum(best, jnp.max(part.reshape(CHUNK // 8, 8, block), axis=0))
+        for c in range(block // SCORE_CHUNK):
+            part = dot(k_buf[h, slot, score_piece(c)], query_t)
+            scores[slot, score_piece(c)] = part
+            best = jnp.maximum(best, jnp.max(part.reshape(SCORE_CHUNK // 8, 8, block), axis=0))
         if slot == FAR:
             best = jnp.where(has_far, best, -jnp.inf)
         return best
@@ -225,12 +229,12 @@
             top = jnp.where(has_far, top, jnp.float32(1e30))
         total = jnp.zeros((8, block), jnp.float32)
         acc = jnp.zeros((HEAD_DIM, block), jnp.float32)
-        for c in range(per_slot):
-            raised = jnp.exp2(scores[slot, piece(c)] * LOG2_SCALE - top)
-            total = total + jnp.sum(raised.reshape(CHUNK // 8, 8, block), axis=0)
+        for c in range(block // SCORE_CHUNK):
+            raised = jnp.exp2(scores[slot, score_piece(c)] * LOG2_SCALE - top)
+            total = total + jnp.sum(raised.reshape(SCORE_CHUNK // 8, 8, block), axis=0)
             low = raised.astype(jnp.bfloat16)
-            weights[slot, piece(c)] = low
-            acc = acc + dot(v_buf[h, slot, piece(c)].T, low)
+            weights[slot, score_piece(c)] = low
+            acc = acc + dot(v_buf[h, slot, score_piece(c)].T, low)
         return total, acc
 
     def slot_grads(h, slot, query, grad, grad_t, row_dot, dk_ref, dv_ref):

time: 55.5 us -> 55.4 us (level)
  no operation moved by 1% of the time
where the time goes in v8:
time: 55.4 us; the launch traced here: 54.8 us
  Pallas kernels  54 us (97%)
  between operations  0.8 us (1%)
    pallas_call x1, Pallas kernels, local(): pl.pallas_call(kernel, in_specs=[whole] * 4, out_specs=[whole] * 4, out_s...  52.7 us
    pallas_call x1, Pallas kernels, local(): pl.pallas_call(hand_over, in_specs=[whole] * 4, out_specs=[whole] * 4, ou...  1.35 us

profile of v8, /device:TPU:16, one launch (start us, length us, event | category | flops | bytes accessed | tf_op | source)
XLA Modules:
  0.0 54.8 jit_solution(13689488583459752891)
XLA Ops:
  0.6 52.7 %shard_map.75 = (bf16[128,2048]{1,0:T(8,128)(2,1)S(1)}, bf16[128,2048]{1,0:T(8,128)(2,1)S(1)}, bf16[128,2048]{1,0:T(8,128)(2,1)S(1)}, bf16[128,2048]{1,0:T(8,128)(2,1)S(1)}) custom-call(bf16[128,2048]{1,0:T(8,128)(2,1)} %q_in.1, bf16[128,2048]{1,0:T(8,128)(2,1)} %k_in.1, bf16[128,2048]{1,0:T(8,128)(2,1)} %v_in.1, bf16[128,2048]{1,0:T(8,128)(2,1)} %g_in.1), custom_call_target="tpu_custom_call" | custom-call | flops 9663676416 | bytes 4194304 | tf_op jit(solution)/shard_map/pallas_call | solution.py:375
  53.3 1.3 %shard_map.76 = (bf16[128,2048]{1,0:T(8,128)(2,1)}, bf16[128,2048]{1,0:T(8,128)(2,1)}, bf16[128,2048]{1,0:T(8,128)(2,1)}, bf16[128,2048]{1,0:T(8,128)(2,1)}) custom-call(bf16[128,2048]{1,0:T(8,128)(2,1)S(1)} %get-tuple-element.8.refs_0_, bf16[128,2048]{1,0:T(8,128)(2,1)S(1)} %get-tuple-element.9.refs_1_, bf16[128,2048]{1,0:T(8,128)(2,1)S(1)} %get-tuple-element.10.refs_2_, ...), custom_call_target="tpu_custom_call" | custom-call | tf_op jit(solution)/shard_map/pallas_call | solution.py:415
